TPU v7x, 32 devices: a whole 2x2x4 slice. The times are simulated.
32 devices in a mesh: ctx: 2 (over core), ex: 16 (over z, y, x).
Axes of the slice: x: 2, y: 2, z: 4, core: 2. Of those that a mesh axis runs over, the one named last changes fastest.
Arguments:
- acts: bfloat16 [16, 256, 8192], P('ex', 'ctx'), may hold values from -6 to 6
- out_grads: bfloat16 [16, 256, 8192], P('ex', 'ctx'), may hold values from -6 to 6
- projections: bfloat16 [2, 8192, 256], P(None, 'ex', 'ctx'), may hold values from -0.0625 to 0.0625
- segments: int32 [16, 256], P('ex', 'ctx'), may hold values from 0 to 3, never falling along the last dimension, each value on 1 to 128 neighbouring positions
- valid: int32 [16, 256], P('ex', 'ctx'), may hold values 0 or 1
- stored: bfloat16 [49152, 8192], P('ex', 'ctx'), may hold values from -60 to 60, as said below
Outputs:
- scores: float32 [64, 49152], P('ctx', 'ex')
Inputs may be any that keep to these rules, and one draw needn't show every extreme that they name: `stored`: finite real values.
All inputs are finite; a program needn't handle non-finite values. No bound on the sum of `valid` on one device may be relied on, other than what follows from the above.
Results may differ from a plain program's by a relative error of at most 0.005.
Values may be sent and summed in bfloat16 or wider, within the bound.
No kernel may reach another device: no remote copies, remote signals or barrier semaphores. Data moves between devices by JAX's collectives and lax.ppermute only.
A program may use at most 128 MiB of HBM per device.

v0:
```python
import math

import jax
import jax.numpy as jnp
from jax import lax
from jax.sharding import PartitionSpec as P

RANK = 32
MODULES = 8
DOCS = 4
STEPS = 4


damping = 0.1
spread = 1.5
epsilon = 1e-06


def shards(acts, out_grads, projections, segments, valid, stored):
    n_ex = lax.axis_size("ex")
    n_ctx = lax.axis_size("ctx")
    columns = lax.all_gather(projections, "ctx", axis=2, tiled=True)
    x_rows = acts[0]
    g_rows = out_grads[0]
    tok_count = x_rows.shape[0]
    col_count = columns.shape[2]
    weight_piece = lax.all_gather(columns, "ex", axis=1, tiled=True)
    x_term = jnp.dot(x_rows, weight_piece[0], preferred_element_type=jnp.float32)
    g_term = jnp.dot(g_rows, weight_piece[1], preferred_element_type=jnp.float32)
    projected = jnp.stack([x_term, g_term]).astype(jnp.bfloat16)
    modules_all = col_count // RANK
    doc_ids = jnp.arange(DOCS, dtype=jnp.int32)
    onehot = ((segments[0][None, :] == doc_ids[:, None]) & (valid[0][None, :] == 1)).astype(
        jnp.bfloat16
    )
    weighted = (onehot[:, :, None] * projected[1][None, :, :]).reshape(
        DOCS, tok_count, modules_all, RANK
    )
    partial_grads = jnp.einsum(
        "qtmi,tmj->qmij",
        weighted,
        projected[0].reshape(tok_count, modules_all, RANK),
        preferred_element_type=jnp.float32,
    ).reshape(DOCS, modules_all * RANK * RANK)
    queries = lax.psum_scatter(partial_grads, "ctx", scatter_dimension=1, tiled=True)
    feat_count = RANK * RANK
    mod_dev = queries.shape[1] // feat_count
    queries = queries.reshape(DOCS, mod_dev, feat_count)
    store_rows = stored.reshape(stored.shape[0], mod_dev, feat_count)
    local_gram = jnp.einsum(
        "smf,smg->mfg", store_rows, store_rows, preferred_element_type=jnp.float32
    )
    total_rows = stored.shape[0] * n_ex
    curvature = lax.psum(local_gram, "ex") / total_rows
    mean_diag = jnp.trace(curvature, axis1=1, axis2=2) / feat_count
    step_size = (1.0 / (spread * (mean_diag + epsilon)))[None, :, None]
    iterate = step_size * queries
    for iteration in range(STEPS):
        applied = (
            jnp.einsum("mfg,qmg->qmf", curvature, iterate, precision=lax.Precision.HIGHEST)
            + damping * mean_diag[None, :, None] * iterate
        )
        iterate = iterate + step_size * (queries - applied)
    precond = lax.all_gather(iterate.astype(jnp.bfloat16), "ex", axis=0, tiled=True)
    query_total = precond.shape[0]
    flat_queries = precond.reshape(query_total, mod_dev * feat_count)
    length_all = tok_count * n_ctx
    score_scale = 1.0 / math.sqrt(MODULES * feat_count * length_all / DOCS)
    query_part = lax.slice_in_dim(
        flat_queries, 0, query_total // n_ctx * lax.axis_size("ctx"), axis=0
    )
    summed_scores = lax.psum_scatter(
        lax.dot_general(
            query_part, stored, (((1,), (1,)), ((), ())), preferred_element_type=jnp.float32
        ),
        "ctx",
        scatter_dimension=0,
        tiled=True,
    )
    return summed_scores * score_scale


def solution(mesh):
    in_specs = (
        P("ex", "ctx", None),
        P("ex", "ctx", None),
        P(None, "ex", "ctx"),
        P("ex", "ctx"),
        P("ex", "ctx"),
        P("ex", "ctx"),
    )
    out_specs = P("ctx", "ex")
    return jax.shard_map(shards, mesh=mesh, in_specs=in_specs, out_specs=out_specs, check_vma=False)
```

profile of v0, /device:TPU:0, one launch (start us, length us, event | category | flops | bytes accessed | tf_op | source)
XLA Modules:
  0.0 761.9 jit_solution(9424018069496284283)
XLA Ops:
  6.5 4.3 all_gather.9
  10.9 0.7 compare_bitcast_fusion
  11.6 0.7 fusion.94
  12.2 113.9 %all-gather.2.cloned.1.call-done = bf16[2,8192,256]{2,1,0:T(8,128)(2,1)} async-done(((bf16[2,512,256]{2,1,0:T(8,128)(2,1)}), bf16[2,8192,256]{2,1,0:T(8,128)(2,1)}) %all-gather.2.cloned.1.call-update) | async-done | bytes 8388624 | tf_op jit(solution)/shard_map/all_gather | solution.py:27
  126.1 2.9 fusion.19
  129.0 0.1 copy.19
  129.2 3.5 fusion.22
  132.8 0.5 convolution_bitcast_fusion
  133.3 4.7 copy.26
  138.0 33.9 %fusion = f32[4,1024,1024]{2,1,0:T(8,128)} fusion(bf16[384,4,8,1024]{3,2,1,0:T(8,128)(2,1)} %bitcast.90), kind=kOutput, calls=%fused_computation | convolution fusion | flops 25769803776 | bytes 41943040 | tf_op jit(solution)/shard_map/smf,smg->mfg/dot_general | solution.py:50
  172.0 0.6 reduce-scatter.5.cloned.1.call-start
  172.6 0.3 iota_compare_fusion
  172.9 2.2 copy.25
  175.1 450.7 %all-reduce.2.cloned.1.call-done = f32[4,1024,1024]{2,1,0:T(8,128)} async-done(((f32[4,1024,1024]{2,1,0:T(8,128)}), f32[4,1024,1024]{2,1,0:T(8,128)}) %all-reduce.2.cloned.1.call-update) | async-done | bytes 16777232 | tf_op jit(solution)/shard_map/psum | solution.py:54
  625.9 8.7 %select_reduce_fusion = f32[4]{0:T(128)S(1)} fusion(f32[4,1024,1024]{2,1,0:T(8,128)} %all-reduce.2.cloned.1.call-done, pred[1024,1024]{1,0:T(8,128)(4,1)S(1)} %iota_compare_fusion), kind=kLoop, calls=%fused_computation.3 | loop fusion | flops 12582908 | bytes 17825808 | tf_op jit(solution)/shard_map/jit(trace)/reduce_sum | solution.py:55
  634.6 17.3 %fusion.85 = f32[4,4,1024]{2,0,1:T(4,128)S(1)} fusion(f32[4,4,1024]{2,0,1:T(4,128)S(1)} %bitcast.95, f32[4,1024,1024]{2,1,0:T(8,128)} %all-reduce.2.cloned.1.call-done, f32[4]{0:T(128)S(1)} %get-tuple-element.6, f32[4]{0:T(128)S(1)} %get-tuple-element.5), kind=kOutput, calls=%fused_computation.46 | convolution fusion | flops 205635584 | bytes 16908320 | tf_op jit(solution)/shard_map/mfg,qmg->qmf/dot_general | solution.py:60
  651.9 13.7 %fusion.73 = f32[4,4,1024]{2,0,1:T(4,128)S(1)} fusion(f32[4,4,1024]{2,0,1:T(4,128)S(1)} %fusion.85, f32[4,4,1024]{2,0,1:T(4,128)S(1)} %bitcast.96, f32[4,1024,1024]{2,1,0:T(8,128)S(1)} %copy-done.2, f32[4]{0:T(128)S(1)} %get-tuple-element.6, f32[4]{0:T(128)S(1)} %get-tuple-element.5), kind=kOutput, calls=%fused_computation.42 | convolution fusion | flops 205602816 | bytes 16973856 | tf_op jit(solution)/shard_map/mfg,qmg->qmf/dot_general | solution.py:60
  665.6 13.9 %fusion.61 = f32[4,4,1024]{2,0,1:T(4,128)S(1)} fusion(f32[4,4,1024]{2,0,1:T(4,128)S(1)} %fusion.73, f32[4,4,1024]{2,0,1:T(4,128)S(1)} %bitcast.97, f32[4,1024,1024]{2,1,0:T(8,128)S(1)} %copy-done.2, f32[4]{0:T(128)S(1)} %get-tuple-element.6, f32[4]{0:T(128)S(1)} %get-tuple-element.5), kind=kOutput, calls=%fused_computation.38 | convolution fusion | flops 205602816 | bytes 16973856 | tf_op jit(solution)/shard_map/mfg,qmg->qmf/dot_general | solution.py:60
  679.5 14.1 %fusion.49 = bf16[4,4,1024]{2,0,1:T(4,128)(2,1)S(1)} fusion(f32[4,4,1024]{2,0,1:T(4,128)S(1)} %fusion.61, f32[4,4,1024]{2,0,1:T(4,128)S(1)} %bitcast.98, f32[4,1024,1024]{2,1,0:T(8,128)S(1)} %copy-done.2, f32[4]{0:T(128)S(1)} %get-tuple-element.6, f32[4]{0:T(128)S(1)} %get-tuple-element.5), kind=kOutput, calls=%fused_computation.34 | convolution fusion | flops 205619200 | bytes 16941088 | tf_op jit(solution)/shard_map/mfg,qmg->qmf/dot_general | solution.py:60
  693.6 41.7 %all_gather.11 = bf16[64,4,1024]{2,1,0:T(4,128)(2,1)S(1)} all-gather(bf16[4,4,1024]{2,1,0:T(4,128)(2,1)S(1)} %copy.22), channel_id=1, replica_groups=mesh['ctx'=2,'ex'=16] {'ex'}, dimensions={0}, use_global_device_ids=true | all-gather | bytes 557056 | tf_op jit(solution)/shard_map/all_gather | solution.py:64
  735.3 0.2 copy.29
  735.5 13.6 %fusion.99 = f32[64,3072]{1,0:T(8,128)} fusion(bf16[64,4096]{1,0:T(8,128)(2,1)S(1)} %bitcast.92, bf16[3072,4096]{1,0:T(8,128)(2,1)} %param.11), kind=kOutput, calls=%fused_computation.64 | convolution fusion | flops 1610612736 | bytes 26476544 | tf_op jit(solution)/shard_map/dot_general | solution.py:73
  749.1 4.3 reduce-scatter.5.cloned.1.call-done
  753.4 1.8 broadcast_multiply_fusion
  (17 shorter events, 0.3 us)
Async XLA Ops:
  6.5 119.6 %copy-start = (bf16[1,128,8192]{2,1,0:T(8,128)(2,1)S(1)}, bf16[1,128,8192]{2,1,0:T(8,128)(2,1)}, u32[]{:S(2)}) copy-start(bf16[1,128,8192]{2,1,0:T(8,128)(2,1)} %param.6) | copy-start | bytes 6291460
  6.5 119.6 %all-gather.2.cloned.1.call-start = ((), (), s32[]{:S(2)}) async-start(), calls=%async_computation.3 | async-start | bytes 8912896 | tf_op jit(solution)/shard_map/all_gather | solution.py:27
  10.9 162.1 %reduce-scatter.7.cloned.1.call-start = ((), (), s32[]{:S(2)}) async-start(), calls=%async_computation.5 | async-start | bytes 6291456
  138.0 487.9 %all-reduce.2.cloned.1.call-start = ((), (), s32[]{:S(2)}) async-start(), calls=%async_computation.2 | async-start | bytes 33554432 | tf_op jit(solution)/shard_map/psum | solution.py:54
  172.0 581.4 %reduce-scatter.5.cloned.1.call-start = ((), (), s32[]{:S(2)}) async-start(), calls=%async_computation.4 | async-start | bytes 1179648 | tf_op jit(solution)/shard_map/reduce_scatter | solution.py:72
  634.6 17.3 %copy-start.2 = (f32[4,1024,1024]{2,1,0:T(8,128)S(1)}, f32[4,1024,1024]{2,1,0:T(8,128)}, u32[]{:S(2)}) copy-start(f32[4,1024,1024]{2,1,0:T(8,128)} %all-reduce.2.cloned.1.call-done) | copy-start | bytes 50331652
  735.5 19.7 %copy-start.1 = (bf16[1,128,8192]{2,1,0:T(8,128)(2,1)S(1)}, bf16[1,128,8192]{2,1,0:T(8,128)(2,1)}, u32[]{:S(2)}) copy-start(bf16[1,128,8192]{2,1,0:T(8,128)(2,1)} %param.6) | copy-start | bytes 6291460
Sparse Core Ops, SparseCore 0:
  11.0 115.1 all-gather.1
  138.1 10.2 reduce-scatter.6
  172.1 453.6 all-reduce.1
  749.3 4.1 reduce-scatter.4
where the time goes:
time: 769 us; the launch traced here: 762 us
  waiting for transfers between devices  569 us (74%)
  matrix products  113 us (15%)
  blocking collectives  46 us (6%)
  between operations  13.4 us (2%)
  other arithmetic  12.1 us (2%)
    psum x1, waiting for transfers between devices, shards(): curvature = lax.psum(local_gram, 'ex') / total_rows  451 us
    all_gather x1, waiting for transfers between devices, shards(): weight_piece = lax.all_gather(columns, 'ex', axis=1, tiled=True)  114 us
    dot_general x4, matrix products, shards(): jnp.einsum('mfg,qmg->qmf', curvature, iterate, precision=lax.Precision.HI...  59 us
    all_gather x1, blocking collectives, shards(): lax.all_gather(iterate.astype(jnp.bfloat16), 'ex', axis=0, tiled=True)  41.7 us
    dot_general x1, matrix products, shards(): jnp.einsum('smf,smg->mfg', store_rows, store_rows, preferred_element_type...  33.9 us
  transfers between devices with their start and end apart: 4, of which 3 were waited for; matrix products, arithmetic and copies ran while one was open for 5% of the time, Pallas kernels for 0%

commit v1 on v0

v1 whole, which is shorter than its diff:
```python
import functools
import math

import jax
import jax.numpy as jnp
from jax import lax
from jax.experimental import pallas as pl
from jax.experimental.pallas import tpu as pltpu
from jax.sharding import PartitionSpec as P

RANK = 32
MODULES = 8
DOCS = 4
STEPS = 4
FEAT = RANK * RANK
HALF = FEAT // 2
BLOCK = FEAT // 4
EXTRA = 16

damping = 0.1
spread = 1.5
epsilon = 1e-06


def gram_kernel(s_ref, out_ref, diag_ref, ab_ref, c_ref):
    k = pl.program_id(1)

    @pl.when(k == 0)
    def _():
        ab_ref[...] = jnp.zeros_like(ab_ref)
        c_ref[...] = jnp.zeros_like(c_ref)

    rows = s_ref[...]
    contract = (((0,), (0,)), ((), ()))
    ab_ref[...] += lax.dot_general(
        rows[:, :HALF], rows, contract, preferred_element_type=jnp.float32
    )
    c_ref[...] += lax.dot_general(
        rows[:, HALF:], rows[:, HALF:], contract, preferred_element_type=jnp.float32
    )

    @pl.when(k == pl.num_programs(1) - 1)
    def _():
        at_row = lax.broadcasted_iota(jnp.int32, (HALF, HALF), 0)
        at_col = lax.broadcasted_iota(jnp.int32, (HALF, HALF), 1)
        a = ab_ref[:, :HALF]
        c = c_ref[...]
        out_ref[0, :HALF] = ab_ref[:, HALF:].astype(jnp.bfloat16)
        out_ref[0, HALF:] = jnp.where(at_row < at_col, a, c).astype(jnp.bfloat16)
        on = at_row == at_col
        diag_ref[0, :, :HALF] = jnp.sum(jnp.where(on, a, 0.0), axis=0, keepdims=True)
        diag_ref[0, :, HALF:] = jnp.sum(jnp.where(on, c, 0.0), axis=0, keepdims=True)


def packed_gram(stored):
    rows, cols = stored.shape
    modules = cols // FEAT
    depth = 1024
    while rows % depth:
        depth //= 2
    return pl.pallas_call(
        gram_kernel,
        grid=(modules, rows // depth),
        in_specs=[pl.BlockSpec((depth, FEAT), lambda m, k: (k, m))],
        out_specs=[
            pl.BlockSpec((1, FEAT, HALF), lambda m, k: (m, 0, 0)),
            pl.BlockSpec((1, 1, FEAT), lambda m, k: (m, 0, 0)),
        ],
        out_shape=[
            jax.ShapeDtypeStruct((modules, FEAT, HALF), jnp.bfloat16),
            jax.ShapeDtypeStruct((modules, 1, FEAT), jnp.float32),
        ],
        scratch_shapes=[
            pltpu.VMEM((HALF, FEAT), jnp.float32),
            pltpu.VMEM((HALF, HALF), jnp.float32),
        ],
        compiler_params=pltpu.CompilerParams(vmem_limit_bytes=32 * 1024 * 1024),
        cost_estimate=pl.CostEstimate(
            flops=2 * rows * FEAT * FEAT * modules * 3 // 4,
            bytes_accessed=rows * cols * 2 + modules * FEAT * HALF * 2,
            transcendentals=0,
        ),
        name="gram",
    )(stored)


def richardson_kernel(total_rows, packed_ref, diag_ref, q_ref, out_ref, full_ref):
    at_row = lax.broadcasted_iota(jnp.int32, (HALF, HALF), 0)
    at_col = lax.broadcasted_iota(jnp.int32, (HALF, HALF), 1)
    both = packed_ref[HALF:].astype(jnp.float32)
    both_t = both.T
    zero = jnp.zeros_like(both)
    above, below = at_row < at_col, at_row > at_col
    full_ref[:HALF, :HALF] = jnp.where(above, both, jnp.where(below, both_t, zero)).astype(jnp.bfloat16)
    full_ref[HALF:, HALF:] = jnp.where(below, both, jnp.where(above, both_t, zero)).astype(jnp.bfloat16)
    cross = packed_ref[:HALF]
    full_ref[:HALF, HALF:] = cross
    full_ref[HALF:, :HALF] = cross.astype(jnp.float32).T.astype(jnp.bfloat16)
    diag = diag_ref[...] / total_rows
    mean_diag = jnp.sum(diag, axis=1, keepdims=True) / FEAT
    step_size = 1.0 / (spread * (mean_diag + epsilon))
    own = diag + damping * mean_diag
    queries = q_ref[...]
    count = queries.shape[0]
    v = step_size * queries
    for _ in range(STEPS):
        high = v.astype(jnp.bfloat16)
        rest = v - high.astype(jnp.float32)
        mid = rest.astype(jnp.bfloat16)
        low = (rest - mid.astype(jnp.float32)).astype(jnp.bfloat16)
        parts = jnp.concatenate([high, mid, low], axis=0)
        off = jnp.dot(parts, full_ref[...], preferred_element_type=jnp.float32)
        off = off[:count] + (off[count : 2 * count] + off[2 * count :])
        v = v + step_size * (queries - (off / total_rows + own * v))
    out_ref[...] = v.astype(jnp.bfloat16)


def precondition(total_rows, packed, diag, queries):
    count = queries.shape[0]
    return pl.pallas_call(
        functools.partial(richardson_kernel, total_rows),
        out_shape=jax.ShapeDtypeStruct((count, FEAT), jnp.bfloat16),
        scratch_shapes=[pltpu.VMEM((FEAT, FEAT), jnp.bfloat16)],
        compiler_params=pltpu.CompilerParams(vmem_limit_bytes=32 * 1024 * 1024),
        cost_estimate=pl.CostEstimate(
            flops=2 * STEPS * 3 * count * FEAT * FEAT, bytes_accessed=4 * FEAT * FEAT, transcendentals=0
        ),
        name="richardson",
    )(packed, diag, queries)


def swapped(value, n_ctx):
    return [value] + [
        lax.ppermute(value, "ctx", [(i, (i + s) % n_ctx) for i in range(n_ctx)])
        for s in range(1, n_ctx)
    ]


def general(acts, out_grads, projections, segments, valid, stored):
    n_ex = lax.axis_size("ex")
    n_ctx = lax.axis_size("ctx")
    tok_count = acts.shape[1]
    mod_dev = projections.shape[2] // RANK
    owners = n_ex // mod_dev
    me = lax.axis_index("ex")

    weights = [lax.all_gather(projections[i], "ex", axis=0, tiled=True) for i in range(2)]
    x_parts = swapped(acts[0], n_ctx)
    g_parts = swapped(out_grads[0], n_ctx)
    marks = swapped(jnp.concatenate([segments, valid], axis=0), n_ctx)

    packed, diag = packed_gram(stored)
    sums = lax.psum_scatter(
        packed.reshape(n_ex, FEAT // owners, HALF), "ex", scatter_dimension=0, tiled=True
    )[0]
    diag = lax.psum(diag, "ex")
    groups = [list(range(m * owners, (m + 1) * owners)) for m in range(mod_dev)]
    packed_mine = lax.all_gather(sums, "ex", axis=0, tiled=True, axis_index_groups=groups)
    my_module = me // owners
    diag_mine = lax.dynamic_index_in_dim(diag, my_module, 0, keepdims=False)

    queries = 0.0
    doc_ids = jnp.arange(DOCS, dtype=jnp.int32)
    for x_rows, g_rows, mark in zip(x_parts, g_parts, marks):
        xp = jnp.dot(x_rows, weights[0], preferred_element_type=jnp.float32).astype(jnp.bfloat16)
        gp = jnp.dot(g_rows, weights[1], preferred_element_type=jnp.float32).astype(jnp.bfloat16)
        onehot = ((mark[0][None, :] == doc_ids[:, None]) & (mark[1][None, :] == 1)).astype(jnp.bfloat16)
        weighted = (onehot[:, :, None] * gp[None, :, :]).reshape(DOCS, tok_count, mod_dev, RANK)
        queries = queries + jnp.einsum(
            "qtmi,tmj->mqij",
            weighted,
            xp.reshape(tok_count, mod_dev, RANK),
            preferred_element_type=jnp.float32,
        )
    queries = queries.reshape(mod_dev, DOCS, FEAT)

    place = lax.rem(me, mod_dev)
    arrived = []
    for j in range(mod_dev):
        module = lax.rem(place + j, mod_dev)
        part = lax.dynamic_index_in_dim(queries, module, 0, keepdims=False)
        pairs = [
            (e, ((e % mod_dev + j) % mod_dev) * owners + e // mod_dev) for e in range(n_ex)
        ]
        arrived.append(lax.ppermute(part, "ex", pairs))
    arrived = jnp.stack(arrived)
    order = lax.rem(my_module - jnp.arange(mod_dev) + mod_dev, mod_dev)
    mine = jnp.take(arrived, order, axis=0).reshape(mod_dev * DOCS, FEAT)

    total_rows = stored.shape[0] * n_ex
    precond = precondition(float(total_rows), packed_mine, diag_mine, mine)

    flat = lax.all_gather(precond, "ex", axis=0, tiled=True).reshape(mod_dev, n_ex * DOCS, FEAT)
    flat = jnp.transpose(flat, (1, 0, 2)).reshape(n_ex * DOCS, mod_dev * FEAT)
    score_scale = 1.0 / math.sqrt(MODULES * FEAT * tok_count * n_ctx / DOCS)
    summed = lax.psum_scatter(
        lax.dot_general(flat, stored, (((1,), (1,)), ((), ())), preferred_element_type=jnp.float32),
        "ctx",
        scatter_dimension=0,
        tiled=True,
    )
    return summed * score_scale


def vmem_params():
    return pltpu.CompilerParams(vmem_limit_bytes=32 * 1024 * 1024)


def small_cost(*arrays):
    return pl.CostEstimate(
        flops=0, bytes_accessed=sum(math.prod(a.shape) * a.dtype.itemsize for a in arrays), transcendentals=0
    )


def rows_of_diag(diag):
    high = diag.astype(jnp.bfloat16)
    rest = diag - high.astype(jnp.float32)
    mid = rest.astype(jnp.bfloat16)
    low = (rest - mid.astype(jnp.float32)).astype(jnp.bfloat16)
    empty = jnp.zeros((EXTRA - 3 * diag.shape[0], HALF), jnp.float32)
    terms = [t.astype(jnp.float32) for t in (high, mid, low)]
    return jnp.concatenate(terms + [empty], axis=0).astype(jnp.bfloat16)


def diag_of_rows(rows):
    terms = rows.astype(jnp.float32)
    return terms[0:2] + (terms[2:4] + terms[4:6])


def block_gram_kernel(ties, meta_ref, s_ref, *refs):
    o0, o1, o2, o3a, o3b, extra_ref, ab_ref, c_ref, pay_ref = refs[ties:]
    k = pl.program_id(0)

    @pl.when(k == 0)
    def _():
        ab_ref[...] = jnp.zeros_like(ab_ref)
        c_ref[...] = jnp.zeros_like(c_ref)

    rows = s_ref[...]
    contract = (((0,), (0,)), ((), ()))
    ab_ref[...] += lax.dot_general(
        rows[:, :HALF], rows, contract, preferred_element_type=jnp.float32
    )
    c_ref[...] += lax.dot_general(
        rows[:, HALF:], rows[:, HALF:], contract, preferred_element_type=jnp.float32
    )

    @pl.when(k == pl.num_programs(0) - 1)
    def _():
        at_row = lax.broadcasted_iota(jnp.int32, (HALF, HALF), 0)
        at_col = lax.broadcasted_iota(jnp.int32, (HALF, HALF), 1)
        a = ab_ref[:, :HALF]
        c = c_ref[...]
        cross = ab_ref[:, HALF:].astype(jnp.bfloat16)
        both = jnp.where(at_row < at_col, a, c).astype(jnp.bfloat16)
        pay_ref[0] = cross[:BLOCK]
        pay_ref[1] = cross[BLOCK:]
        pay_ref[2] = both[:BLOCK]
        pay_ref[3] = both[BLOCK:]
        on = at_row == at_col
        diag_a = jnp.sum(jnp.where(on, a, 0.0), axis=0, keepdims=True)
        diag_c = jnp.sum(jnp.where(on, c, 0.0), axis=0, keepdims=True)
        extra_ref[...] = rows_of_diag(jnp.concatenate([diag_a, diag_c], axis=0))
        o0[...] = pay_ref[meta_ref[1]]
        o1[...] = pay_ref[meta_ref[2]]
        o2[...] = pay_ref[meta_ref[3]]
        o3a[...] = pay_ref[meta_ref[4], : BLOCK // 2]
        o3b[...] = pay_ref[meta_ref[4], BLOCK // 2 :]


def block_gram(stored, module, corner, ties):
    rows = stored.shape[0]
    depth = 1024
    while rows % depth:
        depth //= 2
    meta = jnp.stack([module] + [corner ^ j for j in range(4)]).astype(jnp.int32)
    heights = [BLOCK, BLOCK, BLOCK, BLOCK // 2, BLOCK // 2, EXTRA]
    return pl.pallas_call(
        functools.partial(block_gram_kernel, len(ties)),
        grid_spec=pltpu.PrefetchScalarGridSpec(
            num_scalar_prefetch=1,
            grid=(rows // depth,),
            in_specs=[pl.BlockSpec((depth, FEAT), lambda k, meta: (k, meta[0]))]
            + [pl.BlockSpec(memory_space=pl.ANY)] * len(ties),
            out_specs=[pl.BlockSpec((h, HALF), lambda k, meta: (0, 0)) for h in heights],
            scratch_shapes=[
                pltpu.VMEM((HALF, FEAT), jnp.float32),
                pltpu.VMEM((HALF, HALF), jnp.float32),
                pltpu.VMEM((4, BLOCK, HALF), jnp.bfloat16),
            ],
        ),
        out_shape=[jax.ShapeDtypeStruct((h, HALF), jnp.bfloat16) for h in heights],
        compiler_params=vmem_params(),
        cost_estimate=pl.CostEstimate(
            flops=2 * rows * FEAT * FEAT * 3 // 4,
            bytes_accessed=rows * FEAT * 2 + FEAT * HALF * 2,
            transcendentals=0,
        ),
        name="gram",
    )(meta, stored, *ties)


def pass_kernel(o1, o2, from_x, from_y, for_x, for_y):
    half = BLOCK // 2
    f32 = jnp.float32
    for_x[:half] = o1[:half]
    for_x[half:] = (o1[half:].astype(f32) + from_y[...].astype(f32)).astype(jnp.bfloat16)
    for_y[:half] = (o2[:half].astype(f32) + from_x[...].astype(f32)).astype(jnp.bfloat16)
    for_y[half:] = o2[half:]


def pass_on(o1, o2, from_x, from_y):
    return pl.pallas_call(
        pass_kernel,
        out_shape=[jax.ShapeDtypeStruct(o1.shape, o1.dtype)] * 2,
        compiler_params=vmem_params(),
        cost_estimate=small_cost(o1, o2, o1, o2),
        name="pass_on",
    )(o1, o2, from_x, from_y)


def close_kernel(count, *refs):
    blocks, extra, arrived, out = refs[:3], refs[3], refs[4:-1], refs[-1]
    f32 = jnp.float32
    total = blocks[0][...].astype(f32) + blocks[1][...].astype(f32) + blocks[2][...].astype(f32)
    if not count:
        out[:BLOCK] = total.astype(jnp.bfloat16)
        out[BLOCK:] = extra[...]
        return
    diag = diag_of_rows(extra[...])
    for other in arrived:
        total = total + other[:BLOCK].astype(f32)
        diag = diag + diag_of_rows(other[BLOCK:])
    out[:BLOCK] = total.astype(jnp.bfloat16)
    out[BLOCK:] = rows_of_diag(diag)


def close(o0, got_x, got_y, extra, arrived=()):
    return pl.pallas_call(
        functools.partial(close_kernel, len(arrived)),
        out_shape=jax.ShapeDtypeStruct((BLOCK + EXTRA, HALF), jnp.bfloat16),
        compiler_params=vmem_params(),
        cost_estimate=small_cost(o0, got_x, got_y, *arrived),
        name="close",
    )(o0, got_x, got_y, extra, *arrived)


def project_kernel(has_total, meta_ref, *refs):
    own, across, along, opp0, opp1 = refs[:5]
    rest = refs[5:]
    total_in = None
    if has_total:
        total_in, rest = rest[0], rest[1:]
    out = rest[-1]
    rest = rest[:-1]
    parts = len(rest) // 8
    for which in range(2):
        for part in range(parts):
            total = None
            for corner in range(4):
                block = rest[(part * 2 + which) * 4 + corner][...]
                if corner < 3:
                    piece = (own, across, along)[corner][which]
                else:
                    piece = (opp0, opp1)[which][...]
                term = jnp.dot(block, piece, preferred_element_type=jnp.float32)
                total = term if total is None else total + term
            if has_total:
                total = total + total_in[which, part]
            out[which, part] = total


def project(pieces, x_parts, g_parts, line, corner, total):
    opp0 = pieces[3]
    depth, width = opp0.shape
    tok_count = x_parts[0].shape[0]
    meta = jnp.stack([4 * line + (corner ^ j) for j in range(4)]).astype(jnp.int32)

    def whole(shape):
        return pl.BlockSpec(shape, lambda i, meta: (0,) * len(shape))

    def columns(j):
        return pl.BlockSpec((tok_count, depth), lambda i, meta: (0, meta[j]))

    in_specs = [whole(p.shape) for p in pieces]
    operands = list(pieces)
    if total is not None:
        in_specs.append(whole(total.shape))
        operands.append(total)
    for x_rows, g_rows in zip(x_parts, g_parts):
        for rows in (x_rows, g_rows):
            for j in range(4):
                in_specs.append(columns(j))
                operands.append(rows)
    shape = (2, len(x_parts), tok_count, width)
    return pl.pallas_call(
        functools.partial(project_kernel, total is not None),
        grid_spec=pltpu.PrefetchScalarGridSpec(
            num_scalar_prefetch=1,
            grid=(1,),
            in_specs=in_specs,
            out_specs=whole(shape),
        ),
        out_shape=jax.ShapeDtypeStruct(shape, jnp.float32),
        compiler_params=vmem_params(),
        cost_estimate=pl.CostEstimate(
            flops=2 * 2 * len(x_parts) * tok_count * 4 * depth * width,
            bytes_accessed=2 * (2 * len(x_parts) * tok_count + 2 * width) * 4 * depth,
            transcendentals=0,
        ),
        name="project",
    )(meta, *operands)


def gradient_kernel(meta_ref, total_ref, *refs):
    parts = total_ref.shape[1]
    marks, outs = refs[:parts], refs[parts:]
    width = total_ref.shape[3]
    xp = jnp.concatenate([total_ref[0, p].astype(jnp.bfloat16) for p in range(parts)], axis=0)
    gp = jnp.concatenate([total_ref[1, p].astype(jnp.bfloat16) for p in range(parts)], axis=0)
    tok_count = total_ref.shape[2]
    doc = lax.broadcasted_iota(jnp.int32, (EXTRA, tok_count), 0)
    weight = jnp.concatenate(
        [
            jnp.where((m[0:1, :] == doc) & (m[1:2, :] == 1), 1.0, 0.0).astype(jnp.bfloat16)
            for m in marks
        ],
        axis=1,
    )
    row = lax.broadcasted_iota(jnp.int32, (width, FEAT), 0)
    col = lax.broadcasted_iota(jnp.int32, (width, FEAT), 1)
    for r, out in enumerate(outs):
        at = row - RANK * meta_ref[r]
        pick_x = jnp.where(at == lax.rem(col, RANK), 1.0, 0.0).astype(jnp.bfloat16)
        pick_g = jnp.where(at == col // RANK, 1.0, 0.0).astype(jnp.bfloat16)
        x_wide = jnp.dot(xp, pick_x, preferred_element_type=jnp.float32)
        g_wide = jnp.dot(gp, pick_g, preferred_element_type=jnp.float32)
        product = x_wide * g_wide
        high = product.astype(jnp.bfloat16)
        low = (product - high.astype(jnp.float32)).astype(jnp.bfloat16)
        both = jnp.dot(weight, high, preferred_element_type=jnp.float32)
        both = both + jnp.dot(weight, low, preferred_element_type=jnp.float32)
        out[...] = both[:DOCS]


def gradients(total, marks, line, modules):
    meta = jnp.stack([lax.rem(line + r, modules) for r in range(modules)]).astype(jnp.int32)
    return pl.pallas_call(
        gradient_kernel,
        in_specs=[pl.BlockSpec(memory_space=pltpu.SMEM)]
        + [pl.BlockSpec(memory_space=pltpu.VMEM)] * (1 + len(marks)),
        out_shape=[jax.ShapeDtypeStruct((DOCS, FEAT), jnp.float32)] * modules,
        compiler_params=vmem_params(),
        cost_estimate=pl.CostEstimate(
            flops=4 * modules * 256 * 128 * FEAT, bytes_accessed=4 * FEAT * 128, transcendentals=0
        ),
        name="gradients",
    )(meta, total, *marks)


def corner_richardson_kernel(total_rows, meta_ref, own, across, along, opp_a, opp_b, *refs):
    q_refs, (out_ref, pack_ref, full_ref) = refs[:-3], refs[-3:]
    pack_ref[meta_ref[0]] = own[:BLOCK]
    pack_ref[meta_ref[1]] = across[:BLOCK]
    pack_ref[meta_ref[2]] = along[:BLOCK]
    pack_ref[meta_ref[3], : BLOCK // 2] = opp_a[...]
    pack_ref[meta_ref[3], BLOCK // 2 :] = opp_b[: BLOCK // 2]
    packed = pack_ref[...].reshape(FEAT, HALF)
    at_row = lax.broadcasted_iota(jnp.int32, (HALF, HALF), 0)
    at_col = lax.broadcasted_iota(jnp.int32, (HALF, HALF), 1)
    both = packed[HALF:].astype(jnp.float32)
    both_t = both.T
    zero = jnp.zeros_like(both)
    above, below = at_row < at_col, at_row > at_col
    full_ref[:HALF, :HALF] = jnp.where(above, both, jnp.where(below, both_t, zero)).astype(jnp.bfloat16)
    full_ref[HALF:, HALF:] = jnp.where(below, both, jnp.where(above, both_t, zero)).astype(jnp.bfloat16)
    cross = packed[:HALF]
    full_ref[:HALF, HALF:] = cross
    full_ref[HALF:, :HALF] = cross.astype(jnp.float32).T.astype(jnp.bfloat16)
    diag = diag_of_rows(own[BLOCK:]) + diag_of_rows(across[BLOCK:])
    diag = diag + (diag_of_rows(along[BLOCK:]) + diag_of_rows(opp_b[BLOCK // 2 :]))
    diag = jnp.concatenate([diag[0:1], diag[1:2]], axis=1) / total_rows
    mean_diag = jnp.sum(diag, axis=1, keepdims=True) / FEAT
    step_size = 1.0 / (spread * (mean_diag + epsilon))
    own_diag = diag + damping * mean_diag
    lines = len(q_refs)
    queries = jnp.concatenate([q[...] for q in q_refs], axis=0)
    count = queries.shape[0]
    v = step_size * queries
    for _ in range(STEPS):
        high = v.astype(jnp.bfloat16)
        rest = v - high.astype(jnp.float32)
        mid = rest.astype(jnp.bfloat16)
        low = (rest - mid.astype(jnp.float32)).astype(jnp.bfloat16)
        parts = jnp.concatenate([high, mid, low], axis=0)
        off = jnp.dot(parts, full_ref[...], preferred_element_type=jnp.float32)
        off = off[:count] + (off[count : 2 * count] + off[2 * count :])
        v = v + step_size * (queries - (off / total_rows + own_diag * v))
    to = lax.broadcasted_iota(jnp.int32, (count, count), 0)
    at = lax.broadcasted_iota(jnp.int32, (count, count), 1)
    source = jnp.zeros((count, count), jnp.int32)
    for r in range(lines):
        here = (to >= DOCS * meta_ref[4 + r]) & (to < DOCS * (meta_ref[4 + r] + 1))
        source = jnp.where(here, to + DOCS * (r - meta_ref[4 + r]), source)
    order = jnp.where(at == source, 1.0, 0.0).astype(jnp.bfloat16)
    out_ref[...] = jnp.dot(order, v.astype(jnp.bfloat16), preferred_element_type=jnp.float32).astype(
        jnp.bfloat16
    )


def corner_precondition(total_rows, pieces, corner, line, queries):
    lines = len(queries)
    meta = jnp.stack(
        [corner ^ j for j in range(4)] + [lax.rem(line - r + lines, lines) for r in range(lines)]
    ).astype(jnp.int32)
    count = lines * DOCS
    return pl.pallas_call(
        functools.partial(corner_richardson_kernel, total_rows),
        in_specs=[pl.BlockSpec(memory_space=pltpu.SMEM)]
        + [pl.BlockSpec(memory_space=pltpu.VMEM)] * (5 + lines),
        out_shape=jax.ShapeDtypeStruct((count, FEAT), jnp.bfloat16),
        scratch_shapes=[
            pltpu.VMEM((4, BLOCK, HALF), jnp.bfloat16),
            pltpu.VMEM((FEAT, FEAT), jnp.bfloat16),
        ],
        compiler_params=vmem_params(),
        cost_estimate=pl.CostEstimate(
            flops=2 * STEPS * 3 * count * FEAT * FEAT, bytes_accessed=4 * FEAT * FEAT, transcendentals=0
        ),
        name="richardson",
    )(meta, *pieces, *queries)


def corner_score_kernel(scale, meta_ref, *refs):
    pieces, s_ref, mine_ref, other_ref, flat_ref = refs[:4], refs[4], refs[5], refs[6], refs[7]
    lines, count, _ = pieces[0].shape

    @pl.when(pl.program_id(0) == 0)
    def _():
        for j, piece in enumerate(pieces):
            at = pl.multiple_of(meta_ref[j] * count, count)
            for s in range(lines):
                col = pl.multiple_of(meta_ref[4 + s] * FEAT, FEAT)
                flat_ref[pl.ds(at, count), pl.ds(col, FEAT)] = piece[s]

    scores = lax.dot_general(
        s_ref[...], flat_ref[...], (((1,), (1,)), ((), ())), preferred_element_type=jnp.float32
    )
    scores = scale * scores.T
    rows = [
        scores[k * count + z * DOCS : k * count + (z + 1) * DOCS] for z in range(lines) for k in range(4)
    ]
    half = len(rows) // 2
    low, high = jnp.concatenate(rows[:half], axis=0), jnp.concatenate(rows[half:], axis=0)
    first = meta_ref[4 + lines] == 0
    mine_ref[...] = jnp.where(first, low, high)
    other_ref[...] = jnp.where(first, high, low)


def corner_score(pieces, stored, corner, line, scale):
    lines, count, _ = pieces[0].shape
    rows, width = stored.shape
    total = 4 * count
    tile = 512
    meta = jnp.stack(
        [corner ^ j for j in range(4)]
        + [lax.rem(line - s + lines, lines) for s in range(lines)]
        + [lax.axis_index("ctx")]
    ).astype(jnp.int32)
    shape = (total // 2, rows)
    return pl.pallas_call(
        functools.partial(corner_score_kernel, scale),
        grid_spec=pltpu.PrefetchScalarGridSpec(
            num_scalar_prefetch=1,
            grid=(rows // tile,),
            in_specs=[pl.BlockSpec(p.shape, lambda i, meta: (0, 0, 0)) for p in pieces]
            + [pl.BlockSpec((tile, width), lambda i, meta: (i, 0))],
            out_specs=[pl.BlockSpec((shape[0], tile), lambda i, meta: (0, i))] * 2,
            scratch_shapes=[pltpu.VMEM((total, width), jnp.bfloat16)],
        ),
        out_shape=[jax.ShapeDtypeStruct(shape, jnp.float32)] * 2,
        compiler_params=vmem_params(),
        cost_estimate=pl.CostEstimate(
            flops=2 * total * width * rows, bytes_accessed=2 * rows * width, transcendentals=0
        ),
        name="score",
    )(meta, *pieces, stored)


def to_corner(value, n_ex, bit):
    return lax.ppermute(value, "ex", [(e, e ^ bit) for e in range(n_ex)])


def to_plane(value, n_ex, shift):
    return lax.ppermute(value, "ex", [(e, (e + 4 * shift) % n_ex) for e in range(n_ex)])


def shards(acts, out_grads, projections, segments, valid, stored):
    n_ex = lax.axis_size("ex")
    n_ctx = lax.axis_size("ctx")
    mod_dev = projections.shape[2] // RANK
    if mod_dev != 4 or n_ex != 16 or n_ctx != 2:
        return general(acts, out_grads, projections, segments, valid, stored)
    lines = n_ex // 4
    tok_count = acts.shape[1]
    me = lax.axis_index("ex")
    line, corner = me // 4, lax.rem(me, 4)

    planes = {0: projections}
    for s in (1, 3, 2):
        planes[s] = to_plane(projections, n_ex, s)
    marks = swapped(jnp.concatenate([segments, valid], axis=0), n_ctx)
    across, along, opp0, opp1 = {}, {}, {}, {}
    order = [0, 1, 3, 2]
    grams = {}
    ties = []
    for i, s in enumerate(order):
        across[s] = to_corner(planes[s], n_ex, 1)
        along[s] = to_corner(planes[s], n_ex, 2)
        if i:
            p = order[i - 1]
            opp0[p] = to_corner(along[p][0], n_ex, 1)
            opp1[p] = to_corner(across[p][1], n_ex, 2)
        if i == 2:
            x_parts = swapped(acts[0], n_ctx)
        if i == 3:
            g_parts = swapped(out_grads[0], n_ctx)
        r = (i + 1) % lines
        grams[r] = block_gram(stored, lax.rem(line + r, lines), corner, ties)
        ties = [across[s], along[s]]
        if i:
            ties += [opp0[order[i - 1]], opp1[order[i - 1]]]
        if i < 3:
            ties += [planes[order[i + 1]]]
    last = order[-1]
    opp0[last] = to_corner(along[last][0], n_ex, 1)
    opp1[last] = to_corner(across[last][1], n_ex, 2)

    total = None
    for s in order:
        total = project(
            (planes[s], across[s], along[s], opp0[s], opp1[s]),
            x_parts,
            g_parts,
            lax.rem(line - s + lines, lines),
            corner,
            total,
        )
    docs = gradients(total, marks, line, mod_dev)
    queries = [docs[0]] + [to_plane(docs[s], n_ex, s) for s in range(1, lines)]

    sent = []
    for r in list(range(1, lines)) + [0]:
        o0, o1, o2, o3a, o3b, extra = grams[r]
        from_x = to_corner(o3a, n_ex, 1)
        from_y = to_corner(o3b, n_ex, 2)
        for_x, for_y = pass_on(o1, o2, from_x, from_y)
        got_x = to_corner(for_x, n_ex, 1)
        got_y = to_corner(for_y, n_ex, 2)
        if r:
            sent.append(to_plane(close(o0, got_x, got_y, extra), n_ex, r))
        else:
            kept = close(o0, got_x, got_y, extra, sent)

    kept_x = to_corner(kept, n_ex, 1)
    kept_y = to_corner(kept, n_ex, 2)
    opp_a = to_corner(kept_y[: BLOCK // 2], n_ex, 1)
    opp_b = to_corner(kept_x[BLOCK // 2 :], n_ex, 2)

    total_rows = stored.shape[0] * n_ex
    precond = corner_precondition(
        float(total_rows), (kept, kept_x, kept_y, opp_a, opp_b), corner, line, queries
    )

    stack = jnp.stack([precond] + [to_plane(precond, n_ex, s) for s in range(1, lines)])
    pieces = [stack] + [to_corner(stack, n_ex, bit) for bit in (1, 2, 3)]
    scale = 1.0 / math.sqrt(MODULES * FEAT * tok_count * n_ctx / DOCS)
    mine, other = corner_score(pieces, stored, corner, line, scale)
    return mine + lax.ppermute(other, "ctx", [(0, 1), (1, 0)])


def solution(mesh):
    in_specs = (
        P("ex", "ctx", None),
        P("ex", "ctx", None),
        P(None, "ex", "ctx"),
        P("ex", "ctx"),
        P("ex", "ctx"),
        P("ex", "ctx"),
    )
    out_specs = P("ctx", "ex")
    return jax.shard_map(shards, mesh=mesh, in_specs=in_specs, out_specs=out_specs, check_vma=False)
```

time: 769 us -> 211 us (0.27)
  waiting for transfers between devices: 569 us -> 38.1 us
  matrix products: 113 us -> 0 us
  Pallas kernels: 0 us -> 70.6 us
  starting transfers between devices: 0.65 us -> 63.4 us
  blocking collectives: 46 us -> 0 us
  local copies, waits for them, and re-layouts: 7.29 us -> 33 us
  between operations: 13.4 us -> 0.49 us
    psum x1 -> x0, waiting for transfers between devices: 451 us -> none  [shards(): curvature = lax.psum(local_gram, 'ex') / total_rows]
    all_gather x1 -> x0, waiting for transfers between devices: 114 us -> none  [shards(): weight_piece = lax.all_gather(columns, 'ex', axis=1, tiled=True)]
    dot_general x9 -> x0, matrix products: 113 us -> none  [the longest x4 59 us: shards(): jnp.einsum('mfg,qmg->qmf', curvature, iterate, precision=lax.Precision.HI...]
    pallas_call x0 -> x19, Pallas kernels: none -> 70.6 us  [the longest x4 34 us: block_gram(): pl.pallas_call(functools.partial(block_gram_kernel, len(ties)), grid_spec...]
    ppermute x0 -> x55, starting transfers between devices: none -> 63.4 us  [the longest x39 42.5 us: to_corner(): return lax.ppermute(value, 'ex', [(e, e ^ bit) for e in range(n_ex)])]
    all_gather x2 -> x0, blocking collectives: 46 us -> none  [the longest x1 41.7 us: shards(): lax.all_gather(iterate.astype(jnp.bfloat16), 'ex', axis=0, tiled=True)]
    ppermute x0 -> x55, waiting for transfers between devices: none -> 38.1 us  [the longest x12 20 us: to_plane(): lax.ppermute(value, 'ex', [(e, (e + 4 * shift) % n_ex) for e in range(n_e...]
    unnamed x9 -> x128, local copies, waits for them, and re-layouts: 7.04 us -> 28.2 us
  transfers between devices with their start and end apart: 4 -> 55, of which waited for: 3 -> 16; matrix products, arithmetic and copies ran while one was open for 5% -> 4% of each run, Pallas kernels for 0% -> 26%
where the time goes in v1:
time: 211 us; the launch traced here: 210 us
  Pallas kernels  70.6 us (33%)
  starting transfers between devices  63.4 us (30%)
  waiting for transfers between devices  38.1 us (18%)
  local copies, waits for them, and re-layouts  33 us (16%)
  other arithmetic  4.57 us (2%)
    ppermute x39, starting transfers between devices, to_corner(): return lax.ppermute(value, 'ex', [(e, e ^ bit) for e in range(n_ex)])  42.5 us
    pallas_call x4, Pallas kernels, block_gram(): pl.pallas_call(functools.partial(block_gram_kernel, len(ties)), grid_spec...  34 us
    unnamed x128, local copies, waits for them, and re-layouts  28.2 us
    ppermute x12, starting transfers between devices, to_plane(): lax.ppermute(value, 'ex', [(e, (e + 4 * shift) % n_ex) for e in range(n_e...  20.2 us
    ppermute x12, waiting for transfers between devices, to_plane(): lax.ppermute(value, 'ex', [(e, (e + 4 * shift) % n_ex) for e in range(n_e...  20 us
    ppermute x39, waiting for transfers between devices, to_corner(): return lax.ppermute(value, 'ex', [(e, e ^ bit) for e in range(n_ex)])  16.4 us
    pallas_call x1, Pallas kernels, corner_score(): pl.pallas_call(functools.partial(corner_score_kernel, scale), grid_spec=p...  12.8 us
    pallas_call x4, Pallas kernels, project(): pl.pallas_call(functools.partial(project_kernel, total is not None), grid...  10.6 us
  transfers between devices with their start and end apart: 55, of which 16 were waited for; matrix products, arithmetic and copies ran while one was open for 4% of the time, Pallas kernels for 26%

profile of v1, /device:TPU:0, one launch (start us, length us, event | category | flops | bytes accessed | tf_op | source)
XLA Modules:
  0.0 210.2 jit_solution(12248512415084108865)
XLA Ops:
  0.0 3.0 %collective-permute-start.19 = (bf16[2,512,128]{2,1,0:T(8,128)(2,1)}, bf16[2,512,128]{2,1,0:T(8,128)(2,1)S(1)}, u32[]{:S(2)}, u32[]{:S(2)}) collective-permute-start(bf16[2,512,128]{2,1,0:T(8,128)(2,1)} %refs_0_.1), channel_id=1, source_target_pairs={{0,2},{1,3},{2,0},{3,1},{4,6},{5,7},{6,4},{7,5},{8,10},{9,11},{10,... | collective-permute-start | bytes 786440 | tf_op jit(solution)/shard_map/ppermute | solution.py:591
  3.1 8.2 %gram.5 = (bf16[256,512]{1,0:T(8,128)(2,1)S(1)}, bf16[256,512]{1,0:T(8,128)(2,1)S(1)}, bf16[256,512]{1,0:T(8,128)(2,1)S(1)}, bf16[128,512]{1,0:T(8,128)(2,1)S(1)...) custom-call(s32[5]{0:T(128)S(1)} %stack.170.meta_ref, bf16[3072,4096]{1,0:T(8,128)(2,1)} %refs_4_.1), custom_call_target="tpu_custom_call" | custom-call | flops 4831838208 | bytes 7340032 | tf_op jit(solution)/shard_map/gram/pallas_call | solution.py:278
  14.0 2.1 collective-permute-start.3
  18.1 3.6 %collective-permute-start = (bf16[2,512,128]{2,1,0:T(8,128)(2,1)}, bf16[2,512,128]{2,1,0:T(8,128)(2,1)}, u32[]{:S(2)}, u32[]{:S(2)}) collective-permute-start(bf16[2,512,128]{2,1,0:T(8,128)(2,1)} %refs_0_.1), channel_id=1, source_target_pairs={{0,12},{1,13},{2,14},{3,15},{4,0},{5,1},{6,2},{7,3},{8,4},{9,5},{1... | collective-permute-start | bytes 786440 | tf_op jit(solution)/shard_map/ppermute | solution.py:595
  28.8 8.2 %gram.6 = (bf16[256,512]{1,0:T(8,128)(2,1)S(1)}, bf16[256,512]{1,0:T(8,128)(2,1)S(1)}, bf16[256,512]{1,0:T(8,128)(2,1)S(1)}, bf16[128,512]{1,0:T(8,128)(2,1)S(1)...) custom-call(s32[5]{0:T(128)S(1)} %stack.171.meta_ref, bf16[3072,4096]{1,0:T(8,128)(2,1)} %refs_4_.1, ...), custom_call_target="tpu_custom_call" | custom-call | flops 4831838208 | bytes 7340032 | tf_op jit(solution)/shard_map/gram/pallas_call | solution.py:278
  39.7 4.1 %collective-permute-start.8 = (bf16[2,512,128]{2,1,0:T(8,128)(2,1)}, bf16[2,512,128]{2,1,0:T(8,128)(2,1)S(1)}, u32[]{:S(2)}, u32[]{:S(2)}) collective-permute-start(bf16[2,512,128]{2,1,0:T(8,128)(2,1)} %refs_0_.1), channel_id=1, source_target_pairs={{0,8},{1,9},{2,10},{3,11},{4,12},{5,13},{6,14},{7,15},{8,0},{9,1},... | collective-permute-start | bytes 786440 | tf_op jit(solution)/shard_map/ppermute | solution.py:595
  47.9 8.8 %gram.7 = (bf16[256,512]{1,0:T(8,128)(2,1)S(1)}, bf16[256,512]{1,0:T(8,128)(2,1)S(1)}, bf16[256,512]{1,0:T(8,128)(2,1)S(1)}, bf16[128,512]{1,0:T(8,128)(2,1)}, b...) custom-call(s32[5]{0:T(128)S(1)} %stack.172.meta_ref, bf16[3072,4096]{1,0:T(8,128)(2,1)} %refs_4_.1, ...), custom_call_target="tpu_custom_call" | custom-call | flops 4831838208 | bytes 7340032 | tf_op jit(solution)/shard_map/gram/pallas_call | solution.py:278
  78.4 8.8 %gram.4 = (bf16[256,512]{1,0:T(8,128)(2,1)S(1)}, bf16[256,512]{1,0:T(8,128)(2,1)S(1)}, bf16[256,512]{1,0:T(8,128)(2,1)S(1)}, bf16[128,512]{1,0:T(8,128)(2,1)}, b...) custom-call(s32[5]{0:T(128)S(1)} %copy-done.58, bf16[3072,4096]{1,0:T(8,128)(2,1)} %refs_4_.1, ...), custom_call_target="tpu_custom_call" | custom-call | flops 4831838208 | bytes 7340032 | tf_op jit(solution)/shard_map/gram/pallas_call | solution.py:278
  98.6 6.7 %collective-permute-done.9.from_x = bf16[128,512]{1,0:T(8,128)(2,1)} collective-permute-done((bf16[128,512]{1,0:T(8,128)(2,1)}, bf16[128,512]{1,0:T(8,128)(2,1)}, u32[]{:S(2)}, u32[]{:S(2)}) %collective-permute-start.9) | collective-permute-done | bytes 131104 | tf_op jit(solution)/shard_map/ppermute | solution.py:591
  123.5 6.7 %collective-permute-done.24.refs_5_ = bf16[272,512]{1,0:T(8,128)(2,1)} collective-permute-done((bf16[272,512]{1,0:T(8,128)(2,1)}, bf16[272,512]{1,0:T(8,128)(2,1)}, u32[]{:S(2)}, u32[]{:S(2)}) %collective-permute-start.24) | collective-permute-done | bytes 278560 | tf_op jit(solution)/shard_map/ppermute | solution.py:595
  133.4 5.3 %collective-permute-done.31.refs_6_ = bf16[272,512]{1,0:T(8,128)(2,1)S(1)} collective-permute-done((bf16[272,512]{1,0:T(8,128)(2,1)S(1)}, bf16[272,512]{1,0:T(8,128)(2,1)S(1)}, u32[]{:S(2)}, u32[]{:S(2)}) %collective-permute-start.31) | collective-permute-done | bytes 278560 | tf_op jit(solution)/shard_map/ppermute | solution.py:595
  144.9 4.9 %collective-permute-done.32.across = bf16[272,512]{1,0:T(8,128)(2,1)S(1)} collective-permute-done((bf16[272,512]{1,0:T(8,128)(2,1)S(1)}, bf16[272,512]{1,0:T(8,128)(2,1)S(1)}, u32[]{:S(2)}, u32[]{:S(2)}) %collective-permute-start.32) | collective-permute-done | bytes 278560 | tf_op jit(solution)/shard_map/ppermute | solution.py:591
  149.8 2.4 %collective-permute-start.41 = (bf16[512,128]{1,0:T(8,128)(2,1)S(1)}, bf16[512,128]{1,0:T(8,128)(2,1)S(1)}, u32[]{:S(2)}, u32[]{:S(2)}) collective-permute-start(bf16[512,128]{1,0:T(8,128)(2,1)S(1)} %slice_bitcast_fusion), channel_id=1, source_target_pairs={{0,2},{1,3},{2,0},{3,1},{4,6},{5,7},{6,4},{7,5},{8,10},{9,11},{10,... | collective-permute-start | bytes 393224 | tf_op jit(solution)/shard_map/ppermute | solution.py:591
  155.8 2.7 %project.4.refs_5_ = f32[2,2,128,128]{3,2,1,0:T(8,128)S(1)} custom-call(s32[4]{0:T(128)S(1)} %copy-done.55, bf16[2,512,128]{2,1,0:T(8,128)(2,1)} %refs_0_.1, bf16[2,512,128]{2,1,0:T(8,128)(2,1)S(1)} %collective-permute-done.18.refs_0_.refs_1_, bf16[2,512,128]{2,1,0:T(8,128)(2,1)S(1)} %collective-permute-done.19.refs_1_.refs_2_, ...), custom_call_target="tpu_custom_call" | custom-call | flops 268435456 | bytes 3145728 | tf_op jit(solution)/shard_map/project/pallas_call | solution.py:396
  158.6 2.0 collective-permute-start.34
  160.6 2.6 %project.5.refs_5_ = f32[2,2,128,128]{3,2,1,0:T(8,128)S(1)} custom-call(s32[4]{0:T(128)S(1)} %copy-done.56, bf16[2,512,128]{2,1,0:T(8,128)(2,1)S(1)} %copy-done.3, bf16[2,512,128]{2,1,0:T(8,128)(2,1)S(1)} %collective-permute-done.6.refs_0_.refs_1_, bf16[2,512,128]{2,1,0:T(8,128)(2,1)S(1)} %collective-permute-done.4.refs_1_.refs_2_, ...), custom_call_target="tpu_custom_call" | custom-call | flops 268435456 | bytes 3145728 | tf_op jit(solution)/shard_map/project/pallas_call | solution.py:396
  163.4 2.7 %project.6.refs_5_ = f32[2,2,128,128]{3,2,1,0:T(8,128)S(1)} custom-call(s32[4]{0:T(128)S(1)} %copy-done.57, bf16[2,512,128]{2,1,0:T(8,128)(2,1)} %collective-permute-done.refs_4_.refs_0_, bf16[2,512,128]{2,1,0:T(8,128)(2,1)} %collective-permute-done.1.refs_0_.refs_1_, bf16[2,512,128]{2,1,0:T(8,128)(2,1)S(1)} %collective-permute-done.2.refs_1_.refs_2_, ...), custom_call_target="tpu_custom_call" | custom-call | flops 268435456 | bytes 3145728 | tf_op jit(solution)/shard_map/project/pallas_call | solution.py:396
  166.1 2.6 %project.7.total_ref = f32[2,2,128,128]{3,2,1,0:T(8,128)S(1)} custom-call(s32[4]{0:T(128)S(1)} %pad_add_fusion.2.meta_ref, bf16[2,512,128]{2,1,0:T(8,128)(2,1)S(1)} %copy-done.6, bf16[2,512,128]{2,1,0:T(8,128)(2,1)S(1)} %collective-permute-done.36.refs_1_, bf16[2,512,128]{2,1,0:T(8,128)(2,1)S(1)} %collective-permute-done.37.refs_2_, ...), custom_call_target="tpu_custom_call" | custom-call | flops 268435456 | bytes 3145728 | tf_op jit(solution)/shard_map/project/pallas_call | solution.py:396
  168.7 2.6 %gradients.1 = (f32[4,1024]{1,0:T(4,128)S(1)}, f32[4,1024]{1,0:T(4,128)S(1)}, f32[4,1024]{1,0:T(4,128)S(1)}, f32[4,1024]{1,0:T(4,128)S(1)}) custom-call(s32[4]{0:T(128)S(1)} %copy-done.60, f32[2,2,128,128]{3,2,1,0:T(8,128)S(1)} %project.7.total_ref, s32[2,128]{1,0:T(2,128)S(1)} %copy-done.59, s32[2,128]{1,0:T(2,128)S(1)} %collective-permute-done.44.refs_1_), custom_call_target="tpu_custom_call" | custom-call | flops 536870912 | bytes 524288 | tf_op jit(solution)/shard_map/gradients/pallas_call | solution.py:448
  171.4 3.6 %collective-permute-start.46 = (f32[4,1024]{1,0:T(4,128)S(1)}, f32[4,1024]{1,0:T(4,128)S(1)}, u32[]{:S(2)}, u32[]{:S(2)}) collective-permute-start(f32[4,1024]{1,0:T(4,128)S(1)} %get-tuple-element.77), channel_id=1, source_target_pairs={{0,8},{1,9},{2,10},{3,11},{4,12},{5,13},{6,14},{7,15},{8,0},{9,1},... | collective-permute-start | bytes 49160 | tf_op jit(solution)/shard_map/ppermute | solution.py:595
  178.7 2.8 %richardson.1 = bf16[16,1024]{1,0:T(8,128)(2,1)S(1)} custom-call(s32[8]{0:T(128)S(1)} %stack.167.meta_ref, bf16[272,512]{1,0:T(8,128)(2,1)S(1)} %copy-done.10, bf16[272,512]{1,0:T(8,128)(2,1)S(1)} %copy-done.46, bf16[272,512]{1,0:T(8,128)(2,1)S(1)} %copy-done.48, bf16[128,512]{1,0:T(8,128)(2,1)} %collective-permute-done.34.opp_a, ...), custom_call_target="tpu_custom_call" | custom-call | flops 402653184 | bytes 4194304 | tf_op jit(solution)/shard_map/richardson/pallas_call | solution.py:517
  185.4 2.0 collective-permute-done.48
  188.7 3.1 %collective-permute-start.53 = (bf16[4,16,1024]{2,1,0:T(8,128)(2,1)S(1)}, bf16[4,16,1024]{2,1,0:T(8,128)(2,1)S(1)}, u32[]{:S(2)}, u32[]{:S(2)}) collective-permute-start(bf16[4,16,1024]{2,1,0:T(8,128)(2,1)S(1)} %pad_maximum_fusion.refs_0_), channel_id=1, source_target_pairs={{0,3},{1,2},{2,1},{3,0},{4,7},{5,6},{6,5},{7,4},{8,11},{9,10},{10,... | collective-permute-start | bytes 393224 | tf_op jit(solution)/shard_map/ppermute | solution.py:591
  194.8 12.8 %score.1 = (f32[32,3072]{1,0:T(8,128)S(1)}, f32[32,3072]{1,0:T(8,128)S(1)}) custom-call(s32[9]{0:T(128)S(1)} %stack.166.meta_ref, bf16[4,16,1024]{2,1,0:T(8,128)(2,1)S(1)} %pad_maximum_fusion.refs_0_, bf16[4,16,1024]{2,1,0:T(8,128)(2,1)S(1)} %collective-permute-done.51.refs_1_, bf16[4,16,1024]{2,1,0:T(8,128)(2,1)S(1)} %collective-permute-done.52.refs_2_, ...), custom_call_target="tpu_custom_call" | custom-call | flops 1610612736 | bytes 25165824 | tf_op jit(solution)/shard_map/score/pallas_call | solution.py:571
  (257 shorter events, 97.4 us)
Async XLA Ops:
  0.0 21.8 %collective-permute-start.19 = (bf16[2,512,128]{2,1,0:T(8,128)(2,1)}, bf16[2,512,128]{2,1,0:T(8,128)(2,1)S(1)}, u32[]{:S(2)}, u32[]{:S(2)}) collective-permute-start(bf16[2,512,128]{2,1,0:T(8,128)(2,1)} %refs_0_.1), channel_id=1, source_target_pairs={{0,2},{1,3},{2,0},{3,1},{4,6},{5,7},{6,4},{7,5},{8,10},{9,11},{10,... | collective-permute-start | bytes 786440 | tf_op jit(solution)/shard_map/ppermute | solution.py:591
  18.1 21.6 %collective-permute-start = (bf16[2,512,128]{2,1,0:T(8,128)(2,1)}, bf16[2,512,128]{2,1,0:T(8,128)(2,1)}, u32[]{:S(2)}, u32[]{:S(2)}) collective-permute-start(bf16[2,512,128]{2,1,0:T(8,128)(2,1)} %refs_0_.1), channel_id=1, source_target_pairs={{0,12},{1,13},{2,14},{3,15},{4,0},{5,1},{6,2},{7,3},{8,4},{9,5},{1... | collective-permute-start | bytes 786440 | tf_op jit(solution)/shard_map/ppermute | solution.py:595
  21.8 22.0 %collective-permute-start.25 = (bf16[512,128]{1,0:T(8,128)(2,1)S(1)}, bf16[512,128]{1,0:T(8,128)(2,1)S(1)}, u32[]{:S(2)}, u32[]{:S(2)}) collective-permute-start(bf16[512,128]{1,0:T(8,128)(2,1)S(1)} %slice_bitcast_fusion.5), channel_id=1, source_target_pairs={{0,1},{1,0},{2,3},{3,2},{4,5},{5,4},{6,7},{7,6},{8,9},{9,8},{10,11... | collective-permute-start | bytes 393224 | tf_op jit(solution)/shard_map/ppermute | solution.py:591
  23.7 20.7 %collective-permute-start.26 = (bf16[512,128]{1,0:T(8,128)(2,1)S(1)}, bf16[512,128]{1,0:T(8,128)(2,1)S(1)}, u32[]{:S(2)}, u32[]{:S(2)}) collective-permute-start(bf16[512,128]{1,0:T(8,128)(2,1)S(1)} %slice_bitcast_fusion.4), channel_id=1, source_target_pairs={{0,2},{1,3},{2,0},{3,1},{4,6},{5,7},{6,4},{7,5},{8,10},{9,11},{10,... | collective-permute-start | bytes 393224 | tf_op jit(solution)/shard_map/ppermute | solution.py:591
  25.6 19.2 %collective-permute-start.4 = (bf16[2,512,128]{2,1,0:T(8,128)(2,1)S(1)}, bf16[2,512,128]{2,1,0:T(8,128)(2,1)S(1)}, u32[]{:S(2)}, u32[]{:S(2)}) collective-permute-start(bf16[2,512,128]{2,1,0:T(8,128)(2,1)S(1)} %collective-permute-done.3.refs_2_.refs_0_), channel_id=1, source_target_pairs={{0,2},{1,3},{2,0},{3,1},{4,6},{5,7},{6,4},{7,5},{8,10},{9,11},{10,... | collective-permute-start | bytes 786440 | tf_op jit(solution)/shard_map/ppermute | solution.py:591
  27.3 19.1 %collective-permute-start.6 = (bf16[2,512,128]{2,1,0:T(8,128)(2,1)S(1)}, bf16[2,512,128]{2,1,0:T(8,128)(2,1)S(1)}, u32[]{:S(2)}, u32[]{:S(2)}) collective-permute-start(bf16[2,512,128]{2,1,0:T(8,128)(2,1)S(1)} %collective-permute-done.3.refs_2_.refs_0_), channel_id=1, source_target_pairs={{0,1},{1,0},{2,3},{3,2},{4,5},{5,4},{6,7},{7,6},{8,9},{9,8},{10,11... | collective-permute-start | bytes 786440 | tf_op jit(solution)/shard_map/ppermute | solution.py:591
  39.7 20.4 %collective-permute-start.8 = (bf16[2,512,128]{2,1,0:T(8,128)(2,1)}, bf16[2,512,128]{2,1,0:T(8,128)(2,1)S(1)}, u32[]{:S(2)}, u32[]{:S(2)}) collective-permute-start(bf16[2,512,128]{2,1,0:T(8,128)(2,1)} %refs_0_.1), channel_id=1, source_target_pairs={{0,8},{1,9},{2,10},{3,11},{4,12},{5,13},{6,14},{7,15},{8,0},{9,1},... | collective-permute-start | bytes 786440 | tf_op jit(solution)/shard_map/ppermute | solution.py:595
  43.8 20.8 %collective-permute-start.15 = (bf16[256,512]{1,0:T(8,128)(2,1)S(1)}, bf16[256,512]{1,0:T(8,128)(2,1)S(1)}, u32[]{:S(2)}, u32[]{:S(2)}) collective-permute-start(bf16[256,512]{1,0:T(8,128)(2,1)S(1)} %get-tuple-element.56), channel_id=1, source_target_pairs={{0,1},{1,0},{2,3},{3,2},{4,5},{5,4},{6,7},{7,6},{8,9},{9,8},{10,11... | collective-permute-start | bytes 786440 | tf_op jit(solution)/shard_map/ppermute | solution.py:591
  44.3 22.5 %collective-permute-start.16 = (bf16[256,512]{1,0:T(8,128)(2,1)S(1)}, bf16[256,512]{1,0:T(8,128)(2,1)S(1)}, u32[]{:S(2)}, u32[]{:S(2)}) collective-permute-start(bf16[256,512]{1,0:T(8,128)(2,1)S(1)} %get-tuple-element.57), channel_id=1, source_target_pairs={{0,2},{1,3},{2,0},{3,1},{4,6},{5,7},{6,4},{7,5},{8,10},{9,11},{10,... | collective-permute-start | bytes 786440 | tf_op jit(solution)/shard_map/ppermute | solution.py:591
  44.8 15.8 %collective-permute-start.20 = (bf16[128,512]{1,0:T(8,128)(2,1)S(1)}, bf16[128,512]{1,0:T(8,128)(2,1)S(1)}, u32[]{:S(2)}, u32[]{:S(2)}) collective-permute-start(bf16[128,512]{1,0:T(8,128)(2,1)S(1)} %get-tuple-element.62), channel_id=1, source_target_pairs={{0,1},{1,0},{2,3},{3,2},{4,5},{5,4},{6,7},{7,6},{8,9},{9,8},{10,11... | collective-permute-start | bytes 393224 | tf_op jit(solution)/shard_map/ppermute | solution.py:591
  46.3 15.4 %collective-permute-start.21 = (bf16[128,512]{1,0:T(8,128)(2,1)S(1)}, bf16[128,512]{1,0:T(8,128)(2,1)S(1)}, u32[]{:S(2)}, u32[]{:S(2)}) collective-permute-start(bf16[128,512]{1,0:T(8,128)(2,1)S(1)} %get-tuple-element.63), channel_id=1, source_target_pairs={{0,2},{1,3},{2,0},{3,1},{4,6},{5,7},{6,4},{7,5},{8,10},{9,11},{10,... | collective-permute-start | bytes 393224 | tf_op jit(solution)/shard_map/ppermute | solution.py:591
  68.1 84.1 %collective-permute-start.42 = (bf16[128,8192]{1,0:T(8,128)(2,1)S(1)}, bf16[128,8192]{1,0:T(8,128)(2,1)}, u32[]{:S(2)}, u32[]{:S(2)}) collective-permute-start(bf16[128,8192]{1,0:T(8,128)(2,1)S(1)} %bitcast.48), channel_id=1, source_target_pairs={{0,16},{16,0},{1,17},{17,1},{2,18},{18,2},{3,19},{19,3},{4,20},{20... | collective-permute-start | bytes 6291464 | tf_op jit(solution)/shard_map/ppermute | solution.py:134
  72.6 81.4 %collective-permute-start.43 = (bf16[128,8192]{1,0:T(8,128)(2,1)}, bf16[128,8192]{1,0:T(8,128)(2,1)}, u32[]{:S(2)}, u32[]{:S(2)}) collective-permute-start(bf16[128,8192]{1,0:T(8,128)(2,1)} %bitcast.65), channel_id=1, source_target_pairs={{0,16},{16,0},{1,17},{17,1},{2,18},{18,2},{3,19},{19,3},{4,20},{20... | collective-permute-start | bytes 6291464 | tf_op jit(solution)/shard_map/ppermute | solution.py:134
  73.2 17.4 %collective-permute-start.22 = (bf16[256,512]{1,0:T(8,128)(2,1)S(1)}, bf16[256,512]{1,0:T(8,128)(2,1)S(1)}, u32[]{:S(2)}, u32[]{:S(2)}) collective-permute-start(bf16[256,512]{1,0:T(8,128)(2,1)S(1)} %get-tuple-element.64), channel_id=1, source_target_pairs={{0,1},{1,0},{2,3},{3,2},{4,5},{5,4},{6,7},{7,6},{8,9},{9,8},{10,11... | collective-permute-start | bytes 786440 | tf_op jit(solution)/shard_map/ppermute | solution.py:591
  74.7 19.8 %collective-permute-start.23 = (bf16[256,512]{1,0:T(8,128)(2,1)S(1)}, bf16[256,512]{1,0:T(8,128)(2,1)S(1)}, u32[]{:S(2)}, u32[]{:S(2)}) collective-permute-start(bf16[256,512]{1,0:T(8,128)(2,1)S(1)} %get-tuple-element.65), channel_id=1, source_target_pairs={{0,2},{1,3},{2,0},{3,1},{4,6},{5,7},{6,4},{7,5},{8,10},{9,11},{10,... | collective-permute-start | bytes 786440 | tf_op jit(solution)/shard_map/ppermute | solution.py:591
  75.2 14.1 %collective-permute-start.28 = (bf16[128,512]{1,0:T(8,128)(2,1)}, bf16[128,512]{1,0:T(8,128)(2,1)S(1)}, u32[]{:S(2)}, u32[]{:S(2)}) collective-permute-start(bf16[128,512]{1,0:T(8,128)(2,1)} %copy-done.63), channel_id=1, source_target_pairs={{0,2},{1,3},{2,0},{3,1},{4,6},{5,7},{6,4},{7,5},{8,10},{9,11},{10,... | collective-permute-start | bytes 393224 | tf_op jit(solution)/shard_map/ppermute | solution.py:591
  90.6 26.3 %collective-permute-start.17 = (bf16[272,512]{1,0:T(8,128)(2,1)}, bf16[272,512]{1,0:T(8,128)(2,1)}, u32[]{:S(2)}, u32[]{:S(2)}) collective-permute-start(bf16[272,512]{1,0:T(8,128)(2,1)} %close.4), channel_id=1, source_target_pairs={{0,4},{1,5},{2,6},{3,7},{4,8},{5,9},{6,10},{7,11},{8,12},{9,13},{1... | collective-permute-start | bytes 835592 | tf_op jit(solution)/shard_map/ppermute | solution.py:595
  95.3 21.8 %collective-permute-start.29 = (bf16[256,512]{1,0:T(8,128)(2,1)}, bf16[256,512]{1,0:T(8,128)(2,1)}, u32[]{:S(2)}, u32[]{:S(2)}) collective-permute-start(bf16[256,512]{1,0:T(8,128)(2,1)} %get-tuple-element.72), channel_id=1, source_target_pairs={{0,1},{1,0},{2,3},{3,2},{4,5},{5,4},{6,7},{7,6},{8,9},{9,8},{10,11... | collective-permute-start | bytes 786440 | tf_op jit(solution)/shard_map/ppermute | solution.py:591
  105.3 14.1 %collective-permute-start.30 = (bf16[256,512]{1,0:T(8,128)(2,1)}, bf16[256,512]{1,0:T(8,128)(2,1)}, u32[]{:S(2)}, u32[]{:S(2)}) collective-permute-start(bf16[256,512]{1,0:T(8,128)(2,1)} %copy-done.61), channel_id=1, source_target_pairs={{0,2},{1,3},{2,0},{3,1},{4,6},{5,7},{6,4},{7,5},{8,10},{9,11},{10,... | collective-permute-start | bytes 786440 | tf_op jit(solution)/shard_map/ppermute | solution.py:591
  143.3 15.3 %collective-permute-start.40 = (bf16[512,128]{1,0:T(8,128)(2,1)S(1)}, bf16[512,128]{1,0:T(8,128)(2,1)S(1)}, u32[]{:S(2)}, u32[]{:S(2)}) collective-permute-start(bf16[512,128]{1,0:T(8,128)(2,1)S(1)} %slice_bitcast_fusion.1), channel_id=1, source_target_pairs={{0,1},{1,0},{2,3},{3,2},{4,5},{5,4},{6,7},{7,6},{8,9},{9,8},{10,11... | collective-permute-start | bytes 393224 | tf_op jit(solution)/shard_map/ppermute | solution.py:591
  152.2 13.9 %collective-permute-start.38 = (bf16[512,128]{1,0:T(8,128)(2,1)S(1)}, bf16[512,128]{1,0:T(8,128)(2,1)S(1)}, u32[]{:S(2)}, u32[]{:S(2)}) collective-permute-start(bf16[512,128]{1,0:T(8,128)(2,1)S(1)} %slice_bitcast_fusion.3), channel_id=1, source_target_pairs={{0,1},{1,0},{2,3},{3,2},{4,5},{5,4},{6,7},{7,6},{8,9},{9,8},{10,11... | collective-permute-start | bytes 393224 | tf_op jit(solution)/shard_map/ppermute | solution.py:591
  152.2 13.9 %collective-permute-start.39 = (bf16[512,128]{1,0:T(8,128)(2,1)S(1)}, bf16[512,128]{1,0:T(8,128)(2,1)S(1)}, u32[]{:S(2)}, u32[]{:S(2)}) collective-permute-start(bf16[512,128]{1,0:T(8,128)(2,1)S(1)} %slice_bitcast_fusion.2), channel_id=1, source_target_pairs={{0,2},{1,3},{2,0},{3,1},{4,6},{5,7},{6,4},{7,5},{8,10},{9,11},{10,... | collective-permute-start | bytes 393224 | tf_op jit(solution)/shard_map/ppermute | solution.py:591
  154.0 21.3 %collective-permute-start.35 = (bf16[144,512]{1,0:T(8,128)(2,1)}, bf16[144,512]{1,0:T(8,128)(2,1)}, u32[]{:S(2)}, u32[]{:S(2)}) collective-permute-start(bf16[144,512]{1,0:T(8,128)(2,1)} %slice.45), channel_id=1, source_target_pairs={{0,2},{1,3},{2,0},{3,1},{4,6},{5,7},{6,4},{7,5},{8,10},{9,11},{10,... | collective-permute-start | bytes 442376 | tf_op jit(solution)/shard_map/ppermute | solution.py:591
  158.6 16.7 %collective-permute-start.34 = (bf16[128,512]{1,0:T(8,128)(2,1)}, bf16[128,512]{1,0:T(8,128)(2,1)}, u32[]{:S(2)}, u32[]{:S(2)}) collective-permute-start(bf16[128,512]{1,0:T(8,128)(2,1)} %slice.44), channel_id=1, source_target_pairs={{0,1},{1,0},{2,3},{3,2},{4,5},{5,4},{6,7},{7,6},{8,9},{9,8},{10,11... | collective-permute-start | bytes 393224 | tf_op jit(solution)/shard_map/ppermute | solution.py:591
  (95 other events, 655.9 us)

commit v2 on v1

--- a/solution.py
+++ b/solution.py
@@ -202,8 +202,8 @@
     return summed * score_scale
 
 
-def vmem_params():
-    return pltpu.CompilerParams(vmem_limit_bytes=32 * 1024 * 1024)
+def vmem_params(mib):
+    return pltpu.CompilerParams(vmem_limit_bytes=mib * 1024 * 1024)
 
 
 def small_cost(*arrays):
@@ -229,7 +229,7 @@
 
 def block_gram_kernel(ties, meta_ref, s_ref, *refs):
     o0, o1, o2, o3a, o3b, extra_ref, ab_ref, c_ref, pay_ref = refs[ties:]
-    k = pl.program_id(0)
+    k = pl.program_id(1)
 
     @pl.when(k == 0)
     def _():
@@ -245,7 +245,7 @@
         rows[:, HALF:], rows[:, HALF:], contract, preferred_element_type=jnp.float32
     )
 
-    @pl.when(k == pl.num_programs(0) - 1)
+    @pl.when(k == pl.num_programs(1) - 1)
     def _():
         at_row = lax.broadcasted_iota(jnp.int32, (HALF, HALF), 0)
         at_col = lax.broadcasted_iota(jnp.int32, (HALF, HALF), 1)
@@ -260,156 +260,188 @@
         on = at_row == at_col
         diag_a = jnp.sum(jnp.where(on, a, 0.0), axis=0, keepdims=True)
         diag_c = jnp.sum(jnp.where(on, c, 0.0), axis=0, keepdims=True)
-        extra_ref[...] = rows_of_diag(jnp.concatenate([diag_a, diag_c], axis=0))
-        o0[...] = pay_ref[meta_ref[1]]
-        o1[...] = pay_ref[meta_ref[2]]
-        o2[...] = pay_ref[meta_ref[3]]
-        o3a[...] = pay_ref[meta_ref[4], : BLOCK // 2]
-        o3b[...] = pay_ref[meta_ref[4], BLOCK // 2 :]
-
-
-def block_gram(stored, module, corner, ties):
+        extra_ref[0] = rows_of_diag(jnp.concatenate([diag_a, diag_c], axis=0))
+        o0[0] = pay_ref[meta_ref[2]]
+        o1[0] = pay_ref[meta_ref[3]]
+        o2[0] = pay_ref[meta_ref[4]]
+        o3a[0] = pay_ref[meta_ref[5], : BLOCK // 2]
+        o3b[0] = pay_ref[meta_ref[5], BLOCK // 2 :]
+
+
+def block_gram(stored, modules, corner, ties):
     rows = stored.shape[0]
     depth = 1024
     while rows % depth:
         depth //= 2
-    meta = jnp.stack([module] + [corner ^ j for j in range(4)]).astype(jnp.int32)
+    meta = jnp.stack(modules + [corner ^ j for j in range(4)]).astype(jnp.int32)
     heights = [BLOCK, BLOCK, BLOCK, BLOCK // 2, BLOCK // 2, EXTRA]
+    count = len(modules)
     return pl.pallas_call(
         functools.partial(block_gram_kernel, len(ties)),
         grid_spec=pltpu.PrefetchScalarGridSpec(
             num_scalar_prefetch=1,
-            grid=(rows // depth,),
-            in_specs=[pl.BlockSpec((depth, FEAT), lambda k, meta: (k, meta[0]))]
+            grid=(count, rows // depth),
+            in_specs=[pl.BlockSpec((depth, FEAT), lambda i, k, meta: (k, meta[i]))]
             + [pl.BlockSpec(memory_space=pl.ANY)] * len(ties),
-            out_specs=[pl.BlockSpec((h, HALF), lambda k, meta: (0, 0)) for h in heights],
+            out_specs=[pl.BlockSpec((1, h, HALF), lambda i, k, meta: (i, 0, 0)) for h in heights],
             scratch_shapes=[
                 pltpu.VMEM((HALF, FEAT), jnp.float32),
                 pltpu.VMEM((HALF, HALF), jnp.float32),
                 pltpu.VMEM((4, BLOCK, HALF), jnp.bfloat16),
             ],
         ),
-        out_shape=[jax.ShapeDtypeStruct((h, HALF), jnp.bfloat16) for h in heights],
-        compiler_params=vmem_params(),
+        out_shape=[jax.ShapeDtypeStruct((count, h, HALF), jnp.bfloat16) for h in heights],
+        compiler_params=vmem_params(16),
         cost_estimate=pl.CostEstimate(
-            flops=2 * rows * FEAT * FEAT * 3 // 4,
-            bytes_accessed=rows * FEAT * 2 + FEAT * HALF * 2,
+            flops=2 * count * rows * FEAT * FEAT * 3 // 4,
+            bytes_accessed=count * (rows * FEAT * 2 + FEAT * HALF * 2),
             transcendentals=0,
         ),
         name="gram",
-    )(meta, stored, *ties)
-
-
-def pass_kernel(o1, o2, from_x, from_y, for_x, for_y):
+    )(meta, pltpu.with_memory_space_constraint(stored, pltpu.HBM), *ties)
+
+
+def side_kernel(count, *refs):
+    out = refs[-1]
+    for i in range(count):
+        out[:, i] = refs[i][...]
+
+
+def side_by_side(arrays, tie):
+    whole = pl.BlockSpec(memory_space=pltpu.VMEM)
+    first = arrays[0]
+    return pl.pallas_call(
+        functools.partial(side_kernel, len(arrays)),
+        in_specs=[whole] * len(arrays) + [pl.BlockSpec(memory_space=pl.ANY)],
+        out_shape=jax.ShapeDtypeStruct((first.shape[0], len(arrays)) + first.shape[1:], first.dtype),
+        compiler_params=vmem_params(8),
+        cost_estimate=small_cost(*arrays),
+        name="side_by_side",
+    )(*arrays, tie)
+
+
+def forward_kernel(y0, yb, x0, xb, tie, for_x, for_y):
+    for_x[0] = y0[0]
+    for_x[1:] = yb[0]
+    for_y[0] = x0[0]
+    for_y[1:] = xb[0]
+
+
+def forward(x0, xb, y0, yb, tie):
+    depth, width = x0.shape[1:]
+    count = xb.shape[1]
+    out = jax.ShapeDtypeStruct((count + 1, depth, width), x0.dtype)
+
+    def spec(shape, first):
+        return pl.BlockSpec((1,) + shape[1:], lambda i: (first,) + (0,) * (len(shape) - 1))
+
+    return pl.pallas_call(
+        forward_kernel,
+        grid=(1,),
+        in_specs=[spec(y0.shape, 0), spec(yb.shape, 0), spec(x0.shape, 1), spec(xb.shape, 1)]
+        + [pl.BlockSpec(memory_space=pl.ANY)],
+        out_specs=[pl.BlockSpec(out.shape, lambda i: (0, 0, 0))] * 2,
+        out_shape=[out] * 2,
+        compiler_params=vmem_params(16),
+        cost_estimate=small_cost(x0, xb),
+        name="forward",
+    )(y0, yb, x0, xb, tie)
+
+
+def pass_kernel(o1, o2, from_x, from_y, *refs):
+    for_x, for_y = refs[-2:]
     half = BLOCK // 2
     f32 = jnp.float32
-    for_x[:half] = o1[:half]
-    for_x[half:] = (o1[half:].astype(f32) + from_y[...].astype(f32)).astype(jnp.bfloat16)
-    for_y[:half] = (o2[:half].astype(f32) + from_x[...].astype(f32)).astype(jnp.bfloat16)
-    for_y[half:] = o2[half:]
-
-
-def pass_on(o1, o2, from_x, from_y):
+    for_x[:, :half] = o1[:, :half]
+    for_x[:, half:] = (o1[:, half:].astype(f32) + from_y[...].astype(f32)).astype(jnp.bfloat16)
+    for_y[:, :half] = (o2[:, :half].astype(f32) + from_x[...].astype(f32)).astype(jnp.bfloat16)
+    for_y[:, half:] = o2[:, half:]
+
+
+def pass_on(o1, o2, from_x, from_y, ties=()):
     return pl.pallas_call(
         pass_kernel,
+        in_specs=[pl.BlockSpec(memory_space=pltpu.VMEM)] * 4
+        + [pl.BlockSpec(memory_space=pl.ANY)] * len(ties),
         out_shape=[jax.ShapeDtypeStruct(o1.shape, o1.dtype)] * 2,
-        compiler_params=vmem_params(),
+        compiler_params=vmem_params(8),
         cost_estimate=small_cost(o1, o2, o1, o2),
         name="pass_on",
-    )(o1, o2, from_x, from_y)
-
-
-def close_kernel(count, *refs):
-    blocks, extra, arrived, out = refs[:3], refs[3], refs[4:-1], refs[-1]
+    )(o1, o2, from_x, from_y, *ties)
+
+
+def close_kernel(slots, count, o0, got_x, got_y, extra, *refs):
+    arrived, outs = refs[:count], refs[-len(slots) :]
     f32 = jnp.float32
-    total = blocks[0][...].astype(f32) + blocks[1][...].astype(f32) + blocks[2][...].astype(f32)
-    if not count:
+    for i, out in zip(slots, outs):
+        total = o0[i].astype(f32) + got_x[i].astype(f32) + got_y[i].astype(f32)
+        if not count:
+            out[:BLOCK] = total.astype(jnp.bfloat16)
+            out[BLOCK:] = extra[i]
+            continue
+        diag = diag_of_rows(extra[i])
+        for other in arrived:
+            total = total + other[:BLOCK].astype(f32)
+            diag = diag + diag_of_rows(other[BLOCK:])
         out[:BLOCK] = total.astype(jnp.bfloat16)
-        out[BLOCK:] = extra[...]
-        return
-    diag = diag_of_rows(extra[...])
-    for other in arrived:
-        total = total + other[:BLOCK].astype(f32)
-        diag = diag + diag_of_rows(other[BLOCK:])
-    out[:BLOCK] = total.astype(jnp.bfloat16)
-    out[BLOCK:] = rows_of_diag(diag)
-
-
-def close(o0, got_x, got_y, extra, arrived=()):
-    return pl.pallas_call(
-        functools.partial(close_kernel, len(arrived)),
-        out_shape=jax.ShapeDtypeStruct((BLOCK + EXTRA, HALF), jnp.bfloat16),
-        compiler_params=vmem_params(),
+        out[BLOCK:] = rows_of_diag(diag)
+
+
+def close(o0, got_x, got_y, extra, slots, arrived=(), ties=()):
+    return pl.pallas_call(
+        functools.partial(close_kernel, slots, len(arrived)),
+        in_specs=[pl.BlockSpec(memory_space=pltpu.VMEM)] * (4 + len(arrived))
+        + [pl.BlockSpec(memory_space=pl.ANY)] * len(ties),
+        out_shape=[jax.ShapeDtypeStruct((BLOCK + EXTRA, HALF), jnp.bfloat16)] * len(slots),
+        compiler_params=vmem_params(8),
         cost_estimate=small_cost(o0, got_x, got_y, *arrived),
         name="close",
-    )(o0, got_x, got_y, extra, *arrived)
-
-
-def project_kernel(has_total, meta_ref, *refs):
-    own, across, along, opp0, opp1 = refs[:5]
-    rest = refs[5:]
-    total_in = None
-    if has_total:
-        total_in, rest = rest[0], rest[1:]
-    out = rest[-1]
-    rest = rest[:-1]
-    parts = len(rest) // 8
+    )(o0, got_x, got_y, extra, *arrived, *ties)
+
+
+def project_kernel(meta_ref, own0, own_b, x0, xb, y0, yb, opp_x, opp_y, *refs):
+    rest, out = refs[:-1], refs[-1]
+    parts = len(rest) // 2
+    depth = own0.shape[1]
     for which in range(2):
+        weights = []
+        for r0, rb in ((own0, own_b), (x0, xb), (y0, yb)):
+            weights.append([r0.at[which]] + [rb.at[which, i] for i in range(3)])
+        opp = (opp_x, opp_y)[which]
+        weights.append([opp.at[i] for i in range(4)])
         for part in range(parts):
+            rows = rest[which * parts + part]
             total = None
             for corner in range(4):
-                block = rest[(part * 2 + which) * 4 + corner][...]
-                if corner < 3:
-                    piece = (own, across, along)[corner][which]
-                else:
-                    piece = (opp0, opp1)[which][...]
-                term = jnp.dot(block, piece, preferred_element_type=jnp.float32)
-                total = term if total is None else total + term
-            if has_total:
-                total = total + total_in[which, part]
+                for i in range(4):
+                    at = pl.multiple_of(meta_ref[corner * 4 + i] * depth, depth)
+                    term = jnp.dot(
+                        rows[:, pl.ds(at, depth)],
+                        weights[corner][i][...],
+                        preferred_element_type=jnp.float32,
+                    )
+                    total = term if total is None else total + term
             out[which, part] = total
 
 
-def project(pieces, x_parts, g_parts, line, corner, total):
-    opp0 = pieces[3]
-    depth, width = opp0.shape
+def project(pieces, x_parts, g_parts, planes, corner):
+    width = pieces[0].shape[-1]
     tok_count = x_parts[0].shape[0]
-    meta = jnp.stack([4 * line + (corner ^ j) for j in range(4)]).astype(jnp.int32)
-
-    def whole(shape):
-        return pl.BlockSpec(shape, lambda i, meta: (0,) * len(shape))
-
-    def columns(j):
-        return pl.BlockSpec((tok_count, depth), lambda i, meta: (0, meta[j]))
-
-    in_specs = [whole(p.shape) for p in pieces]
-    operands = list(pieces)
-    if total is not None:
-        in_specs.append(whole(total.shape))
-        operands.append(total)
-    for x_rows, g_rows in zip(x_parts, g_parts):
-        for rows in (x_rows, g_rows):
-            for j in range(4):
-                in_specs.append(columns(j))
-                operands.append(rows)
-    shape = (2, len(x_parts), tok_count, width)
-    return pl.pallas_call(
-        functools.partial(project_kernel, total is not None),
-        grid_spec=pltpu.PrefetchScalarGridSpec(
-            num_scalar_prefetch=1,
-            grid=(1,),
-            in_specs=in_specs,
-            out_specs=whole(shape),
-        ),
-        out_shape=jax.ShapeDtypeStruct(shape, jnp.float32),
-        compiler_params=vmem_params(),
+    meta = jnp.stack([4 * p + (corner ^ j) for j in range(4) for p in planes]).astype(jnp.int32)
+    depth = pieces[0].shape[1]
+    return pl.pallas_call(
+        project_kernel,
+        in_specs=[pl.BlockSpec(memory_space=pltpu.SMEM)]
+        + [pl.BlockSpec(memory_space=pltpu.VMEM)] * (len(pieces) + 2 * len(x_parts)),
+        out_shape=jax.ShapeDtypeStruct((2, len(x_parts), tok_count, width), jnp.float32),
+        compiler_params=vmem_params(24),
         cost_estimate=pl.CostEstimate(
-            flops=2 * 2 * len(x_parts) * tok_count * 4 * depth * width,
-            bytes_accessed=2 * (2 * len(x_parts) * tok_count + 2 * width) * 4 * depth,
+            flops=2 * 2 * len(x_parts) * tok_count * 16 * depth * width,
+            bytes_accessed=2 * (2 * len(x_parts) * tok_count + 2 * width) * 16 * depth,
             transcendentals=0,
         ),
         name="project",
-    )(meta, *operands)
+    )(meta, *pieces, *x_parts, *g_parts)
 
 
 def gradient_kernel(meta_ref, total_ref, *refs):
@@ -450,7 +482,7 @@
         in_specs=[pl.BlockSpec(memory_space=pltpu.SMEM)]
         + [pl.BlockSpec(memory_space=pltpu.VMEM)] * (1 + len(marks)),
         out_shape=[jax.ShapeDtypeStruct((DOCS, FEAT), jnp.float32)] * modules,
-        compiler_params=vmem_params(),
+        compiler_params=vmem_params(16),
         cost_estimate=pl.CostEstimate(
             flops=4 * modules * 256 * 128 * FEAT, bytes_accessed=4 * FEAT * 128, transcendentals=0
         ),
@@ -523,7 +555,7 @@
             pltpu.VMEM((4, BLOCK, HALF), jnp.bfloat16),
             pltpu.VMEM((FEAT, FEAT), jnp.bfloat16),
         ],
-        compiler_params=vmem_params(),
+        compiler_params=vmem_params(16),
         cost_estimate=pl.CostEstimate(
             flops=2 * STEPS * 3 * count * FEAT * FEAT, bytes_accessed=4 * FEAT * FEAT, transcendentals=0
         ),
@@ -561,7 +593,7 @@
     lines, count, _ = pieces[0].shape
     rows, width = stored.shape
     total = 4 * count
-    tile = 512
+    tile = 256
     meta = jnp.stack(
         [corner ^ j for j in range(4)]
         + [lax.rem(line - s + lines, lines) for s in range(lines)]
@@ -579,12 +611,12 @@
             scratch_shapes=[pltpu.VMEM((total, width), jnp.bfloat16)],
         ),
         out_shape=[jax.ShapeDtypeStruct(shape, jnp.float32)] * 2,
-        compiler_params=vmem_params(),
+        compiler_params=vmem_params(24),
         cost_estimate=pl.CostEstimate(
             flops=2 * total * width * rows, bytes_accessed=2 * rows * width, transcendentals=0
         ),
         name="score",
-    )(meta, *pieces, stored)
+    )(meta, *pieces, pltpu.with_memory_space_constraint(stored, pltpu.HBM))
 
 
 def to_corner(value, n_ex, bit):
@@ -606,64 +638,39 @@
     me = lax.axis_index("ex")
     line, corner = me // 4, lax.rem(me, 4)
 
-    planes = {0: projections}
-    for s in (1, 3, 2):
-        planes[s] = to_plane(projections, n_ex, s)
+    def gram(planes, ties):
+        return block_gram(stored, [lax.rem(line + r, lines) for r in planes], corner, ties)
+
+    line1, line3, line2 = (to_plane(projections, n_ex, s) for s in (1, 3, 2))
+    x0, y0 = to_corner(projections, n_ex, 1), to_corner(projections, n_ex, 2)
+    o0, o1, o2, o3a, o3b, extra = gram((1, 2), [])
+    own_b = side_by_side([line1, line3, line2], extra)
+    from_x, from_y = to_corner(o3a, n_ex, 1), to_corner(o3b, n_ex, 2)
+    xb, yb = to_corner(own_b, n_ex, 1), to_corner(own_b, n_ex, 2)
+    p0, p1, p2, p3a, p3b, extra_b = gram((3, 0), [own_b, x0, y0])
+    x_parts = swapped(acts[0], n_ctx)
+    g_parts = swapped(out_grads[0], n_ctx)
     marks = swapped(jnp.concatenate([segments, valid], axis=0), n_ctx)
-    across, along, opp0, opp1 = {}, {}, {}, {}
-    order = [0, 1, 3, 2]
-    grams = {}
-    ties = []
-    for i, s in enumerate(order):
-        across[s] = to_corner(planes[s], n_ex, 1)
-        along[s] = to_corner(planes[s], n_ex, 2)
-        if i:
-            p = order[i - 1]
-            opp0[p] = to_corner(along[p][0], n_ex, 1)
-            opp1[p] = to_corner(across[p][1], n_ex, 2)
-        if i == 2:
-            x_parts = swapped(acts[0], n_ctx)
-        if i == 3:
-            g_parts = swapped(out_grads[0], n_ctx)
-        r = (i + 1) % lines
-        grams[r] = block_gram(stored, lax.rem(line + r, lines), corner, ties)
-        ties = [across[s], along[s]]
-        if i:
-            ties += [opp0[order[i - 1]], opp1[order[i - 1]]]
-        if i < 3:
-            ties += [planes[order[i + 1]]]
-    last = order[-1]
-    opp0[last] = to_corner(along[last][0], n_ex, 1)
-    opp1[last] = to_corner(across[last][1], n_ex, 2)
-
-    total = None
-    for s in order:
-        total = project(
-            (planes[s], across[s], along[s], opp0[s], opp1[s]),
-            x_parts,
-            g_parts,
-            lax.rem(line - s + lines, lines),
-            corner,
-            total,
-        )
+    for_x, for_y = pass_on(o1, o2, from_x, from_y, (extra_b, x_parts[1], g_parts[1]))
+    got_x, got_y = to_corner(for_x, n_ex, 1), to_corner(for_y, n_ex, 2)
+    from_xb, from_yb = to_corner(p3a, n_ex, 1), to_corner(p3b, n_ex, 2)
+    opp_x, opp_y = forward(x0, xb, y0, yb, for_x)
+    opp_x, opp_y = to_corner(opp_x, n_ex, 1), to_corner(opp_y, n_ex, 2)
+
+    planes = [lax.rem(line - s + lines, lines) for s in (0, 1, 3, 2)]
+    total = project((projections, own_b, x0, xb, y0, yb, opp_x, opp_y), x_parts, g_parts, planes, corner)
     docs = gradients(total, marks, line, mod_dev)
     queries = [docs[0]] + [to_plane(docs[s], n_ex, s) for s in range(1, lines)]
 
-    sent = []
-    for r in list(range(1, lines)) + [0]:
-        o0, o1, o2, o3a, o3b, extra = grams[r]
-        from_x = to_corner(o3a, n_ex, 1)
-        from_y = to_corner(o3b, n_ex, 2)
-        for_x, for_y = pass_on(o1, o2, from_x, from_y)
-        got_x = to_corner(for_x, n_ex, 1)
-        got_y = to_corner(for_y, n_ex, 2)
-        if r:
-            sent.append(to_plane(close(o0, got_x, got_y, extra), n_ex, r))
-        else:
-            kept = close(o0, got_x, got_y, extra, sent)
-
-    kept_x = to_corner(kept, n_ex, 1)
-    kept_y = to_corner(kept, n_ex, 2)
+    message1, message2 = close(o0, got_x, got_y, extra, (0, 1))
+    for_xb, for_yb = pass_on(p1, p2, from_xb, from_yb, (got_x, got_y))
+    got_xb, got_yb = to_corner(for_xb, n_ex, 1), to_corner(for_yb, n_ex, 2)
+    sent = [to_plane(message1, n_ex, 1), to_plane(message2, n_ex, 2)]
+    (message3,) = close(p0, got_xb, got_yb, extra_b, (0,), (), (docs[0],))
+    sent.append(to_plane(message3, n_ex, 3))
+    (kept,) = close(p0, got_xb, got_yb, extra_b, (1,), sent, queries[1:])
+
+    kept_x, kept_y = to_corner(kept, n_ex, 1), to_corner(kept, n_ex, 2)
     opp_a = to_corner(kept_y[: BLOCK // 2], n_ex, 1)
     opp_b = to_corner(kept_x[BLOCK // 2 :], n_ex, 2)
 

time: 211 us -> 173 us (0.82)
  starting transfers between devices: 63.4 us -> 45.9 us
  local copies, waits for them, and re-layouts: 33 us -> 15.9 us
  waiting for transfers between devices: 38.1 us -> 48 us
  Pallas kernels: 70.6 us -> 61.4 us
  other arithmetic: 4.57 us -> 0.89 us
    ppermute x39 -> x21, waiting for transfers between devices: 16.4 us -> 32.5 us  [to_corner(): return lax.ppermute(value, 'ex', [(e, e ^ bit) for e in range(n_ex)])]
    ppermute x39 -> x21, starting transfers between devices: 42.5 us -> 27.4 us  [to_corner(): return lax.ppermute(value, 'ex', [(e, e ^ bit) for e in range(n_ex)])]
    unnamed x128 -> x62, local copies, waits for them, and re-layouts: 28.2 us -> 15.4 us
    pallas_call x12 -> x8, Pallas kernels: 18.3 us -> 10.9 us  [the longest x1 4.41 us: project(): pl.pallas_call(project_kernel, in_specs=[pl.BlockSpec(memory_space=pltpu....]
    ppermute x12, waiting for transfers between devices: 20 us -> 13.8 us  [to_plane(): lax.ppermute(value, 'ex', [(e, (e + 4 * shift) % n_ex) for e in range(n_e...]
    pallas_call x4 -> x2, Pallas kernels: 34 us -> 29.2 us  [block_gram(): pl.pallas_call(functools.partial(block_gram_kernel, len(ties)), grid_spec...]
    pallas_call x1, Pallas kernels: 12.8 us -> 16.2 us  [corner_score(): pl.pallas_call(functools.partial(corner_score_kernel, scale), grid_spec=p...]
    ppermute x12, starting transfers between devices: 20.2 us -> 17.8 us  [to_plane(): lax.ppermute(value, 'ex', [(e, (e + 4 * shift) % n_ex) for e in range(n_e...]
  transfers between devices with their start and end apart: 55 -> 37, of which waited for: 16 -> 14; matrix products, arithmetic and copies ran while one was open for 4% -> 0% of each run, Pallas kernels for 26% -> 24%
where the time goes in v2:
time: 173 us; the launch traced here: 172 us
  Pallas kernels  61.4 us (35%)
  waiting for transfers between devices  48 us (28%)
  starting transfers between devices  45.9 us (27%)
  local copies, waits for them, and re-layouts  15.9 us (9%)
    ppermute x21, waiting for transfers between devices, to_corner(): return lax.ppermute(value, 'ex', [(e, e ^ bit) for e in range(n_ex)])  32.5 us
    pallas_call x2, Pallas kernels, block_gram(): pl.pallas_call(functools.partial(block_gram_kernel, len(ties)), grid_spec...  29.2 us
    ppermute x21, starting transfers between devices, to_corner(): return lax.ppermute(value, 'ex', [(e, e ^ bit) for e in range(n_ex)])  27.4 us
    ppermute x12, starting transfers between devices, to_plane(): lax.ppermute(value, 'ex', [(e, (e + 4 * shift) % n_ex) for e in range(n_e...  17.8 us
    pallas_call x1, Pallas kernels, corner_score(): pl.pallas_call(functools.partial(corner_score_kernel, scale), grid_spec=p...  16.2 us
    unnamed x62, local copies, waits for them, and re-layouts  15.4 us
    ppermute x12, waiting for transfers between devices, to_plane(): lax.ppermute(value, 'ex', [(e, (e + 4 * shift) % n_ex) for e in range(n_e...  13.8 us
    pallas_call x1, Pallas kernels, project(): pl.pallas_call(project_kernel, in_specs=[pl.BlockSpec(memory_space=pltpu....  4.41 us
  transfers between devices with their start and end apart: 37, of which 14 were waited for; matrix products, arithmetic and copies ran while one was open for 0% of the time, Pallas kernels for 24%

profile of v2, /device:TPU:0, one launch (start us, length us, event | category | flops | bytes accessed | tf_op | source)
XLA Modules:
  0.0 172.4 jit_solution(10013773029305818574)
XLA Ops:
  0.5 3.0 %collective-permute-start = (bf16[2,512,128]{2,1,0:T(8,128)(2,1)}, bf16[2,512,128]{2,1,0:T(8,128)(2,1)S(1)}, u32[]{:S(2)}, u32[]{:S(2)}) collective-permute-start(bf16[2,512,128]{2,1,0:T(8,128)(2,1)} %own0.1), channel_id=1, source_target_pairs={{0,4},{1,5},{2,6},{3,7},{4,8},{5,9},{6,10},{7,11},{8,12},{9,13},{1... | collective-permute-start | bytes 786440 | tf_op jit(solution)/shard_map/ppermute | solution.py:627
  3.5 2.0 %collective-permute-start.1 = (bf16[2,512,128]{2,1,0:T(8,128)(2,1)}, bf16[2,512,128]{2,1,0:T(8,128)(2,1)S(1)}, u32[]{:S(2)}, u32[]{:S(2)}) collective-permute-start(bf16[2,512,128]{2,1,0:T(8,128)(2,1)} %own0.1), channel_id=1, source_target_pairs={{0,12},{1,13},{2,14},{3,15},{4,0},{5,1},{6,2},{7,3},{8,4},{9,5},{1... | collective-permute-start | bytes 786440 | tf_op jit(solution)/shard_map/ppermute | solution.py:627
  6.7 15.0 %gram.2 = (bf16[2,256,512]{2,1,0:T(8,128)(2,1)S(1)}, bf16[2,256,512]{2,1,0:T(8,128)(2,1)S(1)}, bf16[2,256,512]{2,1,0:T(8,128)(2,1)S(1)}, bf16[2,128,512]{2,1,0:T...) custom-call(s32[6]{0:T(128)S(1)} %stack.147.meta_ref, bf16[3072,4096]{1,0:T(8,128)(2,1)} %refs_4_.1), custom_call_target="tpu_custom_call" | custom-call | flops 9663676416 | bytes 14680064 | tf_op jit(solution)/shard_map/gram/pallas_call | solution.py:279
  36.5 2.9 %collective-permute-done.7.from_x = bf16[2,128,512]{2,1,0:T(8,128)(2,1)} collective-permute-done((bf16[2,128,512]{2,1,0:T(8,128)(2,1)}, bf16[2,128,512]{2,1,0:T(8,128)(2,1)}, u32[]{:S(2)}, u32[]{:S(2)}) %collective-permute-start.7) | collective-permute-done | bytes 262176 | tf_op jit(solution)/shard_map/ppermute | solution.py:623
  40.8 14.3 %gram.3 = (bf16[2,256,512]{2,1,0:T(8,128)(2,1)S(1)}, bf16[2,256,512]{2,1,0:T(8,128)(2,1)S(1)}, bf16[2,256,512]{2,1,0:T(8,128)(2,1)S(1)}, bf16[2,128,512]{2,1,0:T...) custom-call(s32[6]{0:T(128)S(1)} %stack.146.meta_ref, bf16[3072,4096]{1,0:T(8,128)(2,1)} %refs_4_.1, ...), custom_call_target="tpu_custom_call" | custom-call | flops 9663676416 | bytes 14680064 | tf_op jit(solution)/shard_map/gram/pallas_call | solution.py:279
  63.3 13.7 %collective-permute-done.5.from_x = bf16[2,128,512]{2,1,0:T(8,128)(2,1)S(1)} collective-permute-done((bf16[2,128,512]{2,1,0:T(8,128)(2,1)S(1)}, bf16[2,128,512]{2,1,0:T(8,128)(2,1)S(1)}, u32[]{:S(2)}, u32[]{:S(2)}) %collective-permute-start.5) | collective-permute-done | bytes 262176 | tf_op jit(solution)/shard_map/ppermute | solution.py:623
  84.5 3.8 %collective-permute-done.19.opp_x = bf16[4,512,128]{2,1,0:T(8,128)(2,1)} collective-permute-done((bf16[4,512,128]{2,1,0:T(8,128)(2,1)}, bf16[4,512,128]{2,1,0:T(8,128)(2,1)}, u32[]{:S(2)}, u32[]{:S(2)}) %collective-permute-start.19) | collective-permute-done | bytes 524320 | tf_op jit(solution)/shard_map/ppermute | solution.py:623
  88.3 2.9 %collective-permute-start.15 = (bf16[272,512]{1,0:T(8,128)(2,1)S(1)}, bf16[272,512]{1,0:T(8,128)(2,1)S(1)}, u32[]{:S(2)}, u32[]{:S(2)}) collective-permute-start(bf16[272,512]{1,0:T(8,128)(2,1)S(1)} %get-tuple-element.47), channel_id=1, source_target_pairs={{0,4},{1,5},{2,6},{3,7},{4,8},{5,9},{6,10},{7,11},{8,12},{9,13},{1... | collective-permute-start | bytes 835592 | tf_op jit(solution)/shard_map/ppermute | solution.py:627
  92.2 1.9 %collective-permute-start.16 = (bf16[272,512]{1,0:T(8,128)(2,1)S(1)}, bf16[272,512]{1,0:T(8,128)(2,1)S(1)}, u32[]{:S(2)}, u32[]{:S(2)}) collective-permute-start(bf16[272,512]{1,0:T(8,128)(2,1)S(1)} %get-tuple-element.48), channel_id=1, source_target_pairs={{0,8},{1,9},{2,10},{3,11},{4,12},{5,13},{6,14},{7,15},{8,0},{9,1},... | collective-permute-start | bytes 835592 | tf_op jit(solution)/shard_map/ppermute | solution.py:627
  99.2 4.4 %project.1.total_ref = f32[2,2,128,128]{3,2,1,0:T(8,128)S(1)} custom-call(s32[16]{0:T(128)S(1)} %stack.165.meta_ref, bf16[2,512,128]{2,1,0:T(8,128)(2,1)} %own0.1, bf16[2,3,512,128]{3,2,1,0:T(8,128)(2,1)S(1)} %side_by_side.1.refs_0_.own_b, bf16[2,512,128]{2,1,0:T(8,128)(2,1)S(1)} %copy-done.12, bf16[2,3,512,128]{3,2,1,0:T(8,128)(2,1)S(1)} %copy-done.1, ...), custom_call_target="tpu_custom_call" | custom-call | flops 1073741824 | bytes 12582912 | tf_op jit(solution)/shard_map/project/pallas_call | solution.py:432
  103.6 2.6 %gradients.1 = (f32[4,1024]{1,0:T(4,128)S(1)}, f32[4,1024]{1,0:T(4,128)S(1)}, f32[4,1024]{1,0:T(4,128)S(1)}, f32[4,1024]{1,0:T(4,128)S(1)}) custom-call(s32[4]{0:T(128)S(1)} %pad_add_fusion.1.meta_ref, f32[2,2,128,128]{3,2,1,0:T(8,128)S(1)} %project.1.total_ref, s32[2,128]{1,0:T(2,128)S(1)} %pad_add_fusion.refs_0_, s32[2,128]{1,0:T(2,128)S(1)} %collective-permute-done.21.refs_1_), custom_call_target="tpu_custom_call" | custom-call | flops 536870912 | bytes 524288 | tf_op jit(solution)/shard_map/gradients/pallas_call | solution.py:480
  107.6 1.9 %collective-permute-start.22 = (bf16[272,512]{1,0:T(8,128)(2,1)S(1)}, bf16[272,512]{1,0:T(8,128)(2,1)S(1)}, u32[]{:S(2)}, u32[]{:S(2)}) collective-permute-start(bf16[272,512]{1,0:T(8,128)(2,1)S(1)} %close.4), channel_id=1, source_target_pairs={{0,12},{1,13},{2,14},{3,15},{4,0},{5,1},{6,2},{7,3},{8,4},{9,5},{1... | collective-permute-start | bytes 835592 | tf_op jit(solution)/shard_map/ppermute | solution.py:627
  110.7 4.3 %collective-permute-done.23.refs_3_.refs_1_ = f32[4,1024]{1,0:T(4,128)S(1)} collective-permute-done((f32[4,1024]{1,0:T(4,128)S(1)}, f32[4,1024]{1,0:T(4,128)S(1)}, u32[]{:S(2)}, u32[]{:S(2)}) %collective-permute-start.23) | collective-permute-done | bytes 16416 | tf_op jit(solution)/shard_map/ppermute | solution.py:627
  115.0 3.7 %collective-permute-done.25.refs_5_.refs_3_ = f32[4,1024]{1,0:T(4,128)S(1)} collective-permute-done((f32[4,1024]{1,0:T(4,128)S(1)}, f32[4,1024]{1,0:T(4,128)S(1)}, u32[]{:S(2)}, u32[]{:S(2)}) %collective-permute-start.25) | collective-permute-done | bytes 16416 | tf_op jit(solution)/shard_map/ppermute | solution.py:627
  120.2 1.8 %collective-permute-start.26 = (bf16[272,512]{1,0:T(8,128)(2,1)S(1)}, bf16[272,512]{1,0:T(8,128)(2,1)S(1)}, u32[]{:S(2)}, u32[]{:S(2)}) collective-permute-start(bf16[272,512]{1,0:T(8,128)(2,1)S(1)} %close.5.own), channel_id=1, source_target_pairs={{0,1},{1,0},{2,3},{3,2},{4,5},{5,4},{6,7},{7,6},{8,9},{9,8},{10,11... | collective-permute-start | bytes 835592 | tf_op jit(solution)/shard_map/ppermute | solution.py:623
  123.5 3.3 %collective-permute-done.26.across = bf16[272,512]{1,0:T(8,128)(2,1)S(1)} collective-permute-done((bf16[272,512]{1,0:T(8,128)(2,1)S(1)}, bf16[272,512]{1,0:T(8,128)(2,1)S(1)}, u32[]{:S(2)}, u32[]{:S(2)}) %collective-permute-start.26) | collective-permute-done | bytes 278560 | tf_op jit(solution)/shard_map/ppermute | solution.py:623
  126.8 1.8 %collective-permute-start.29 = (bf16[144,512]{1,0:T(8,128)(2,1)S(1)}, bf16[144,512]{1,0:T(8,128)(2,1)S(1)}, u32[]{:S(2)}, u32[]{:S(2)}) collective-permute-start(bf16[144,512]{1,0:T(8,128)(2,1)S(1)} %slice.9), channel_id=1, source_target_pairs={{0,2},{1,3},{2,0},{3,1},{4,6},{5,7},{6,4},{7,5},{8,10},{9,11},{10,... | collective-permute-start | bytes 442376 | tf_op jit(solution)/shard_map/ppermute | solution.py:623
  130.2 3.4 %collective-permute-done.28.opp_a = bf16[128,512]{1,0:T(8,128)(2,1)S(1)} collective-permute-done((bf16[128,512]{1,0:T(8,128)(2,1)S(1)}, bf16[128,512]{1,0:T(8,128)(2,1)S(1)}, u32[]{:S(2)}, u32[]{:S(2)}) %collective-permute-start.28) | collective-permute-done | bytes 131104 | tf_op jit(solution)/shard_map/ppermute | solution.py:623
  133.6 2.4 %richardson.1 = bf16[16,1024]{1,0:T(8,128)(2,1)S(1)} custom-call(s32[8]{0:T(128)S(1)} %stack.144.meta_ref, bf16[272,512]{1,0:T(8,128)(2,1)S(1)} %close.5.own, bf16[272,512]{1,0:T(8,128)(2,1)S(1)} %collective-permute-done.26.across, bf16[272,512]{1,0:T(8,128)(2,1)S(1)} %collective-permute-done.27.along, bf16[128,512]{1,0:T(8,128)(2,1)S(1)} %collective-permute-done.28.opp_a, ...), custom_call_target="tpu_custom_call" | custom-call | flops 402653184 | bytes 4194304 | tf_op jit(solution)/shard_map/richardson/pallas_call | solution.py:549
  136.0 2.1 %collective-permute-start.32 = (bf16[16,1024]{1,0:T(8,128)(2,1)S(1)}, bf16[16,1024]{1,0:T(8,128)(2,1)S(1)}, u32[]{:S(2)}, u32[]{:S(2)}) collective-permute-start(bf16[16,1024]{1,0:T(8,128)(2,1)S(1)} %richardson.1), channel_id=1, source_target_pairs={{0,12},{1,13},{2,14},{3,15},{4,0},{5,1},{6,2},{7,3},{8,4},{9,5},{1... | collective-permute-start | bytes 98312 | tf_op jit(solution)/shard_map/ppermute | solution.py:627
  140.3 2.7 %collective-permute-done.31 = bf16[16,1024]{1,0:T(8,128)(2,1)S(1)} collective-permute-done((bf16[16,1024]{1,0:T(8,128)(2,1)S(1)}, bf16[16,1024]{1,0:T(8,128)(2,1)S(1)}, u32[]{:S(2)}, u32[]{:S(2)}) %collective-permute-start.31) | collective-permute-done | bytes 32800 | tf_op jit(solution)/shard_map/ppermute | solution.py:627
  143.1 2.5 %collective-permute-done.30 = bf16[16,1024]{1,0:T(8,128)(2,1)S(1)} collective-permute-done((bf16[16,1024]{1,0:T(8,128)(2,1)S(1)}, bf16[16,1024]{1,0:T(8,128)(2,1)S(1)}, u32[]{:S(2)}, u32[]{:S(2)}) %collective-permute-start.30) | collective-permute-done | bytes 32800 | tf_op jit(solution)/shard_map/ppermute | solution.py:627
  150.7 2.9 %collective-permute-done.34.refs_2_ = bf16[4,16,1024]{2,1,0:T(8,128)(2,1)S(1)} collective-permute-done((bf16[4,16,1024]{2,1,0:T(8,128)(2,1)S(1)}, bf16[4,16,1024]{2,1,0:T(8,128)(2,1)S(1)}, u32[]{:S(2)}, u32[]{:S(2)}) %collective-permute-start.34) | collective-permute-done | bytes 131104 | tf_op jit(solution)/shard_map/ppermute | solution.py:623
  153.6 16.2 %score.1 = (f32[32,3072]{1,0:T(8,128)S(1)}, f32[32,3072]{1,0:T(8,128)S(1)}) custom-call(s32[9]{0:T(128)S(1)} %stack.143.meta_ref, bf16[4,16,1024]{2,1,0:T(8,128)(2,1)S(1)} %pad_maximum_fusion.refs_0_, bf16[4,16,1024]{2,1,0:T(8,128)(2,1)S(1)} %collective-permute-done.33.refs_1_, bf16[4,16,1024]{2,1,0:T(8,128)(2,1)S(1)} %collective-permute-done.34.refs_2_, ...), custom_call_target="tpu_custom_call" | custom-call | flops 1610612736 | bytes 25165824 | tf_op jit(solution)/shard_map/score/pallas_call | solution.py:603
  (136 shorter events, 56.3 us)
Async XLA Ops:
  0.0 55.1 %collective-permute-start.9 = (bf16[128,8192]{1,0:T(8,128)(2,1)}, bf16[128,8192]{1,0:T(8,128)(2,1)S(1)}, u32[]{:S(2)}, u32[]{:S(2)}) collective-permute-start(bf16[128,8192]{1,0:T(8,128)(2,1)} %bitcast.32), channel_id=1, source_target_pairs={{0,16},{16,0},{1,17},{17,1},{2,18},{18,2},{3,19},{19,3},{4,20},{20... | collective-permute-start | bytes 6291464 | tf_op jit(solution)/shard_map/ppermute | solution.py:134
  0.5 54.7 %collective-permute-start.10 = (bf16[128,8192]{1,0:T(8,128)(2,1)}, bf16[128,8192]{1,0:T(8,128)(2,1)}, u32[]{:S(2)}, u32[]{:S(2)}) collective-permute-start(bf16[128,8192]{1,0:T(8,128)(2,1)} %bitcast.34), channel_id=1, source_target_pairs={{0,16},{16,0},{1,17},{17,1},{2,18},{18,2},{3,19},{19,3},{4,20},{20... | collective-permute-start | bytes 6291464 | tf_op jit(solution)/shard_map/ppermute | solution.py:134
  0.5 24.2 %collective-permute-start = (bf16[2,512,128]{2,1,0:T(8,128)(2,1)}, bf16[2,512,128]{2,1,0:T(8,128)(2,1)S(1)}, u32[]{:S(2)}, u32[]{:S(2)}) collective-permute-start(bf16[2,512,128]{2,1,0:T(8,128)(2,1)} %own0.1), channel_id=1, source_target_pairs={{0,4},{1,5},{2,6},{3,7},{4,8},{5,9},{6,10},{7,11},{8,12},{9,13},{1... | collective-permute-start | bytes 786440 | tf_op jit(solution)/shard_map/ppermute | solution.py:627
  3.5 23.4 %collective-permute-start.1 = (bf16[2,512,128]{2,1,0:T(8,128)(2,1)}, bf16[2,512,128]{2,1,0:T(8,128)(2,1)S(1)}, u32[]{:S(2)}, u32[]{:S(2)}) collective-permute-start(bf16[2,512,128]{2,1,0:T(8,128)(2,1)} %own0.1), channel_id=1, source_target_pairs={{0,12},{1,13},{2,14},{3,15},{4,0},{5,1},{6,2},{7,3},{8,4},{9,5},{1... | collective-permute-start | bytes 786440 | tf_op jit(solution)/shard_map/ppermute | solution.py:627
  5.6 23.6 %collective-permute-start.2 = (bf16[2,512,128]{2,1,0:T(8,128)(2,1)}, bf16[2,512,128]{2,1,0:T(8,128)(2,1)S(1)}, u32[]{:S(2)}, u32[]{:S(2)}) collective-permute-start(bf16[2,512,128]{2,1,0:T(8,128)(2,1)} %own0.1), channel_id=1, source_target_pairs={{0,8},{1,9},{2,10},{3,11},{4,12},{5,13},{6,14},{7,15},{8,0},{9,1},... | collective-permute-start | bytes 786440 | tf_op jit(solution)/shard_map/ppermute | solution.py:627
  25.4 8.8 %collective-permute-start.3 = (bf16[2,512,128]{2,1,0:T(8,128)(2,1)}, bf16[2,512,128]{2,1,0:T(8,128)(2,1)S(1)}, u32[]{:S(2)}, u32[]{:S(2)}) collective-permute-start(bf16[2,512,128]{2,1,0:T(8,128)(2,1)} %own0.1), channel_id=1, source_target_pairs={{0,1},{1,0},{2,3},{3,2},{4,5},{5,4},{6,7},{7,6},{8,9},{9,8},{10,11... | collective-permute-start | bytes 786440 | tf_op jit(solution)/shard_map/ppermute | solution.py:623
  27.7 8.3 %collective-permute-start.4 = (bf16[2,512,128]{2,1,0:T(8,128)(2,1)}, bf16[2,512,128]{2,1,0:T(8,128)(2,1)S(1)}, u32[]{:S(2)}, u32[]{:S(2)}) collective-permute-start(bf16[2,512,128]{2,1,0:T(8,128)(2,1)} %own0.1), channel_id=1, source_target_pairs={{0,2},{1,3},{2,0},{3,1},{4,6},{5,7},{6,4},{7,5},{8,10},{9,11},{10,... | collective-permute-start | bytes 786440 | tf_op jit(solution)/shard_map/ppermute | solution.py:623
  29.9 9.5 %collective-permute-start.7 = (bf16[2,128,512]{2,1,0:T(8,128)(2,1)}, bf16[2,128,512]{2,1,0:T(8,128)(2,1)}, u32[]{:S(2)}, u32[]{:S(2)}) collective-permute-start(bf16[2,128,512]{2,1,0:T(8,128)(2,1)} %get-tuple-element.39), channel_id=1, source_target_pairs={{0,1},{1,0},{2,3},{3,2},{4,5},{5,4},{6,7},{7,6},{8,9},{9,8},{10,11... | collective-permute-start | bytes 786440 | tf_op jit(solution)/shard_map/ppermute | solution.py:623
  34.3 20.8 %collective-permute-start.8 = (bf16[2,128,512]{2,1,0:T(8,128)(2,1)}, bf16[2,128,512]{2,1,0:T(8,128)(2,1)S(1)}, u32[]{:S(2)}, u32[]{:S(2)}) collective-permute-start(bf16[2,128,512]{2,1,0:T(8,128)(2,1)} %copy-done.28), channel_id=1, source_target_pairs={{0,2},{1,3},{2,0},{3,1},{4,6},{5,7},{6,4},{7,5},{8,10},{9,11},{10,... | collective-permute-start | bytes 786440 | tf_op jit(solution)/shard_map/ppermute | solution.py:623
  35.9 23.2 %collective-permute-start.17 = (bf16[2,3,512,128]{3,2,1,0:T(8,128)(2,1)S(1)}, bf16[2,3,512,128]{3,2,1,0:T(8,128)(2,1)S(1)}, u32[]{:S(2)}, u32[]{:S(2)}) collective-permute-start(bf16[2,3,512,128]{3,2,1,0:T(8,128)(2,1)S(1)} %side_by_side.1.refs_0_.own_b), channel_id=1, source_target_pairs={{0,1},{1,0},{2,3},{3,2},{4,5},{5,4},{6,7},{7,6},{8,9},{9,8},{10,11... | collective-permute-start | bytes 2359304 | tf_op jit(solution)/shard_map/ppermute | solution.py:623
  39.4 21.3 %collective-permute-start.18 = (bf16[2,3,512,128]{3,2,1,0:T(8,128)(2,1)S(1)}, bf16[2,3,512,128]{3,2,1,0:T(8,128)(2,1)S(1)}, u32[]{:S(2)}, u32[]{:S(2)}) collective-permute-start(bf16[2,3,512,128]{3,2,1,0:T(8,128)(2,1)S(1)} %side_by_side.1.refs_0_.own_b), channel_id=1, source_target_pairs={{0,2},{1,3},{2,0},{3,1},{4,6},{5,7},{6,4},{7,5},{8,10},{9,11},{10,... | collective-permute-start | bytes 2359304 | tf_op jit(solution)/shard_map/ppermute | solution.py:623
  56.4 21.2 %collective-permute-start.11 = (bf16[2,256,512]{2,1,0:T(8,128)(2,1)S(1)}, bf16[2,256,512]{2,1,0:T(8,128)(2,1)S(1)}, u32[]{:S(2)}, u32[]{:S(2)}) collective-permute-start(bf16[2,256,512]{2,1,0:T(8,128)(2,1)S(1)} %get-tuple-element.42.tie), channel_id=1, source_target_pairs={{0,1},{1,0},{2,3},{3,2},{4,5},{5,4},{6,7},{7,6},{8,9},{9,8},{10,11... | collective-permute-start | bytes 1572872 | tf_op jit(solution)/shard_map/ppermute | solution.py:623
  58.0 19.6 %collective-permute-start.12 = (bf16[2,256,512]{2,1,0:T(8,128)(2,1)S(1)}, bf16[2,256,512]{2,1,0:T(8,128)(2,1)S(1)}, u32[]{:S(2)}, u32[]{:S(2)}) collective-permute-start(bf16[2,256,512]{2,1,0:T(8,128)(2,1)S(1)} %get-tuple-element.43), channel_id=1, source_target_pairs={{0,2},{1,3},{2,0},{3,1},{4,6},{5,7},{6,4},{7,5},{8,10},{9,11},{10,... | collective-permute-start | bytes 1572872 | tf_op jit(solution)/shard_map/ppermute | solution.py:623
  58.5 18.5 %collective-permute-start.5 = (bf16[2,128,512]{2,1,0:T(8,128)(2,1)S(1)}, bf16[2,128,512]{2,1,0:T(8,128)(2,1)S(1)}, u32[]{:S(2)}, u32[]{:S(2)}) collective-permute-start(bf16[2,128,512]{2,1,0:T(8,128)(2,1)S(1)} %get-tuple-element.35), channel_id=1, source_target_pairs={{0,1},{1,0},{2,3},{3,2},{4,5},{5,4},{6,7},{7,6},{8,9},{9,8},{10,11... | collective-permute-start | bytes 786440 | tf_op jit(solution)/shard_map/ppermute | solution.py:623
  59.2 18.4 %collective-permute-start.6 = (bf16[2,128,512]{2,1,0:T(8,128)(2,1)S(1)}, bf16[2,128,512]{2,1,0:T(8,128)(2,1)S(1)}, u32[]{:S(2)}, u32[]{:S(2)}) collective-permute-start(bf16[2,128,512]{2,1,0:T(8,128)(2,1)S(1)} %get-tuple-element.36), channel_id=1, source_target_pairs={{0,2},{1,3},{2,0},{3,1},{4,6},{5,7},{6,4},{7,5},{8,10},{9,11},{10,... | collective-permute-start | bytes 786440 | tf_op jit(solution)/shard_map/ppermute | solution.py:623
  61.8 26.6 %collective-permute-start.19 = (bf16[4,512,128]{2,1,0:T(8,128)(2,1)}, bf16[4,512,128]{2,1,0:T(8,128)(2,1)}, u32[]{:S(2)}, u32[]{:S(2)}) collective-permute-start(bf16[4,512,128]{2,1,0:T(8,128)(2,1)} %get-tuple-element.49), channel_id=1, source_target_pairs={{0,1},{1,0},{2,3},{3,2},{4,5},{5,4},{6,7},{7,6},{8,9},{9,8},{10,11... | collective-permute-start | bytes 1572872 | tf_op jit(solution)/shard_map/ppermute | solution.py:623
  77.0 15.2 %collective-permute-start.20 = (bf16[4,512,128]{2,1,0:T(8,128)(2,1)}, bf16[4,512,128]{2,1,0:T(8,128)(2,1)}, u32[]{:S(2)}, u32[]{:S(2)}) collective-permute-start(bf16[4,512,128]{2,1,0:T(8,128)(2,1)} %get-tuple-element.50), channel_id=1, source_target_pairs={{0,2},{1,3},{2,0},{3,1},{4,6},{5,7},{6,4},{7,5},{8,10},{9,11},{10,... | collective-permute-start | bytes 1572872 | tf_op jit(solution)/shard_map/ppermute | solution.py:623
  78.8 27.4 %collective-permute-start.13 = (bf16[2,256,512]{2,1,0:T(8,128)(2,1)}, bf16[2,256,512]{2,1,0:T(8,128)(2,1)}, u32[]{:S(2)}, u32[]{:S(2)}) collective-permute-start(bf16[2,256,512]{2,1,0:T(8,128)(2,1)} %get-tuple-element.44), channel_id=1, source_target_pairs={{0,1},{1,0},{2,3},{3,2},{4,5},{5,4},{6,7},{7,6},{8,9},{9,8},{10,11... | collective-permute-start | bytes 1572872 | tf_op jit(solution)/shard_map/ppermute | solution.py:623
  80.3 25.9 %collective-permute-start.14 = (bf16[2,256,512]{2,1,0:T(8,128)(2,1)}, bf16[2,256,512]{2,1,0:T(8,128)(2,1)}, u32[]{:S(2)}, u32[]{:S(2)}) collective-permute-start(bf16[2,256,512]{2,1,0:T(8,128)(2,1)} %get-tuple-element.45), channel_id=1, source_target_pairs={{0,2},{1,3},{2,0},{3,1},{4,6},{5,7},{6,4},{7,5},{8,10},{9,11},{10,... | collective-permute-start | bytes 1572872 | tf_op jit(solution)/shard_map/ppermute | solution.py:623
  81.8 21.8 %collective-permute-start.21 = (s32[2,128]{1,0:T(2,128)S(1)}, s32[2,128]{1,0:T(2,128)S(1)}, u32[]{:S(2)}, u32[]{:S(2)}) collective-permute-start(s32[2,128]{1,0:T(2,128)S(1)} %pad_add_fusion.refs_0_), channel_id=1, source_target_pairs={{0,16},{16,0},{1,17},{17,1},{2,18},{18,2},{3,19},{19,3},{4,20},{20... | collective-permute-start | bytes 3080 | tf_op jit(solution)/shard_map/ppermute | solution.py:134
  88.3 30.4 %collective-permute-start.15 = (bf16[272,512]{1,0:T(8,128)(2,1)S(1)}, bf16[272,512]{1,0:T(8,128)(2,1)S(1)}, u32[]{:S(2)}, u32[]{:S(2)}) collective-permute-start(bf16[272,512]{1,0:T(8,128)(2,1)S(1)} %get-tuple-element.47), channel_id=1, source_target_pairs={{0,4},{1,5},{2,6},{3,7},{4,8},{5,9},{6,10},{7,11},{8,12},{9,13},{1... | collective-permute-start | bytes 835592 | tf_op jit(solution)/shard_map/ppermute | solution.py:627
  92.2 26.6 %collective-permute-start.16 = (bf16[272,512]{1,0:T(8,128)(2,1)S(1)}, bf16[272,512]{1,0:T(8,128)(2,1)S(1)}, u32[]{:S(2)}, u32[]{:S(2)}) collective-permute-start(bf16[272,512]{1,0:T(8,128)(2,1)S(1)} %get-tuple-element.48), channel_id=1, source_target_pairs={{0,8},{1,9},{2,10},{3,11},{4,12},{5,13},{6,14},{7,15},{8,0},{9,1},... | collective-permute-start | bytes 835592 | tf_op jit(solution)/shard_map/ppermute | solution.py:627
  107.6 11.2 %collective-permute-start.22 = (bf16[272,512]{1,0:T(8,128)(2,1)S(1)}, bf16[272,512]{1,0:T(8,128)(2,1)S(1)}, u32[]{:S(2)}, u32[]{:S(2)}) collective-permute-start(bf16[272,512]{1,0:T(8,128)(2,1)S(1)} %close.4), channel_id=1, source_target_pairs={{0,12},{1,13},{2,14},{3,15},{4,0},{5,1},{6,2},{7,3},{8,4},{9,5},{1... | collective-permute-start | bytes 835592 | tf_op jit(solution)/shard_map/ppermute | solution.py:627
  126.8 6.8 %collective-permute-start.29 = (bf16[144,512]{1,0:T(8,128)(2,1)S(1)}, bf16[144,512]{1,0:T(8,128)(2,1)S(1)}, u32[]{:S(2)}, u32[]{:S(2)}) collective-permute-start(bf16[144,512]{1,0:T(8,128)(2,1)S(1)} %slice.9), channel_id=1, source_target_pairs={{0,2},{1,3},{2,0},{3,1},{4,6},{5,7},{6,4},{7,5},{8,10},{9,11},{10,... | collective-permute-start | bytes 442376 | tf_op jit(solution)/shard_map/ppermute | solution.py:623
  (44 other events, 287.5 us)

commit v3 on v2

--- a/solution.py
+++ b/solution.py
@@ -307,17 +307,17 @@
         out[:, i] = refs[i][...]
 
 
-def side_by_side(arrays, tie):
+def side_by_side(arrays, ties):
     whole = pl.BlockSpec(memory_space=pltpu.VMEM)
     first = arrays[0]
     return pl.pallas_call(
         functools.partial(side_kernel, len(arrays)),
-        in_specs=[whole] * len(arrays) + [pl.BlockSpec(memory_space=pl.ANY)],
+        in_specs=[whole] * len(arrays) + [pl.BlockSpec(memory_space=pl.ANY)] * len(ties),
         out_shape=jax.ShapeDtypeStruct((first.shape[0], len(arrays)) + first.shape[1:], first.dtype),
         compiler_params=vmem_params(8),
         cost_estimate=small_cost(*arrays),
         name="side_by_side",
-    )(*arrays, tie)
+    )(*arrays, *ties)
 
 
 def forward_kernel(y0, yb, x0, xb, tie, for_x, for_y):
@@ -564,7 +564,7 @@
 
 
 def corner_score_kernel(scale, meta_ref, *refs):
-    pieces, s_ref, mine_ref, other_ref, flat_ref = refs[:4], refs[4], refs[5], refs[6], refs[7]
+    pieces, streams, (mine_ref, other_ref, flat_ref) = refs[:4], refs[4:-3], refs[-3:]
     lines, count, _ = pieces[0].shape
 
     @pl.when(pl.program_id(0) == 0)
@@ -572,12 +572,14 @@
         for j, piece in enumerate(pieces):
             at = pl.multiple_of(meta_ref[j] * count, count)
             for s in range(lines):
-                col = pl.multiple_of(meta_ref[4 + s] * FEAT, FEAT)
-                flat_ref[pl.ds(at, count), pl.ds(col, FEAT)] = piece[s]
-
-    scores = lax.dot_general(
-        s_ref[...], flat_ref[...], (((1,), (1,)), ((), ())), preferred_element_type=jnp.float32
-    )
+                flat_ref[meta_ref[4 + s], pl.ds(at, count)] = piece[s]
+
+    scores = None
+    for m, s_ref in enumerate(streams):
+        term = lax.dot_general(
+            s_ref[...], flat_ref[m], (((1,), (1,)), ((), ())), preferred_element_type=jnp.float32
+        )
+        scores = term if scores is None else scores + term
     scores = scale * scores.T
     rows = [
         scores[k * count + z * DOCS : k * count + (z + 1) * DOCS] for z in range(lines) for k in range(4)
@@ -593,22 +595,28 @@
     lines, count, _ = pieces[0].shape
     rows, width = stored.shape
     total = 4 * count
-    tile = 256
+    tile = 512
+    modules = width // FEAT
     meta = jnp.stack(
         [corner ^ j for j in range(4)]
         + [lax.rem(line - s + lines, lines) for s in range(lines)]
         + [lax.axis_index("ctx")]
     ).astype(jnp.int32)
     shape = (total // 2, rows)
+
+    def module_columns(m):
+        return pl.BlockSpec((tile, FEAT), lambda i, meta: (i, m))
+
+    stored = pltpu.with_memory_space_constraint(stored, pltpu.HBM)
     return pl.pallas_call(
         functools.partial(corner_score_kernel, scale),
         grid_spec=pltpu.PrefetchScalarGridSpec(
             num_scalar_prefetch=1,
             grid=(rows // tile,),
             in_specs=[pl.BlockSpec(p.shape, lambda i, meta: (0, 0, 0)) for p in pieces]
-            + [pl.BlockSpec((tile, width), lambda i, meta: (i, 0))],
+            + [module_columns(m) for m in range(modules)],
             out_specs=[pl.BlockSpec((shape[0], tile), lambda i, meta: (0, i))] * 2,
-            scratch_shapes=[pltpu.VMEM((total, width), jnp.bfloat16)],
+            scratch_shapes=[pltpu.VMEM((modules, total, FEAT), jnp.bfloat16)],
         ),
         out_shape=[jax.ShapeDtypeStruct(shape, jnp.float32)] * 2,
         compiler_params=vmem_params(24),
@@ -616,7 +624,7 @@
             flops=2 * total * width * rows, bytes_accessed=2 * rows * width, transcendentals=0
         ),
         name="score",
-    )(meta, *pieces, pltpu.with_memory_space_constraint(stored, pltpu.HBM))
+    )(meta, *pieces, *[stored] * modules)
 
 
 def to_corner(value, n_ex, bit):
@@ -644,12 +652,12 @@
     line1, line3, line2 = (to_plane(projections, n_ex, s) for s in (1, 3, 2))
     x0, y0 = to_corner(projections, n_ex, 1), to_corner(projections, n_ex, 2)
     o0, o1, o2, o3a, o3b, extra = gram((1, 2), [])
-    own_b = side_by_side([line1, line3, line2], extra)
+    own_b = side_by_side([line1, line3, line2], [extra, x0, y0])
+    x_rows, g_rows, _ = lax.optimization_barrier((acts[0], out_grads[0], own_b))
+    x_parts, g_parts = swapped(x_rows, n_ctx), swapped(g_rows, n_ctx)
     from_x, from_y = to_corner(o3a, n_ex, 1), to_corner(o3b, n_ex, 2)
     xb, yb = to_corner(own_b, n_ex, 1), to_corner(own_b, n_ex, 2)
     p0, p1, p2, p3a, p3b, extra_b = gram((3, 0), [own_b, x0, y0])
-    x_parts = swapped(acts[0], n_ctx)
-    g_parts = swapped(out_grads[0], n_ctx)
     marks = swapped(jnp.concatenate([segments, valid], axis=0), n_ctx)
     for_x, for_y = pass_on(o1, o2, from_x, from_y, (extra_b, x_parts[1], g_parts[1]))
     got_x, got_y = to_corner(for_x, n_ex, 1), to_corner(for_y, n_ex, 2)
@@ -666,9 +674,9 @@
     for_xb, for_yb = pass_on(p1, p2, from_xb, from_yb, (got_x, got_y))
     got_xb, got_yb = to_corner(for_xb, n_ex, 1), to_corner(for_yb, n_ex, 2)
     sent = [to_plane(message1, n_ex, 1), to_plane(message2, n_ex, 2)]
-    (message3,) = close(p0, got_xb, got_yb, extra_b, (0,), (), (docs[0],))
+    (message3,) = close(p0, got_xb, got_yb, extra_b, (0,))
     sent.append(to_plane(message3, n_ex, 3))
-    (kept,) = close(p0, got_xb, got_yb, extra_b, (1,), sent, queries[1:])
+    (kept,) = close(p0, got_xb, got_yb, extra_b, (1,), sent, (docs[0],))
 
     kept_x, kept_y = to_corner(kept, n_ex, 1), to_corner(kept, n_ex, 2)
     opp_a = to_corner(kept_y[: BLOCK // 2], n_ex, 1)

time: 173 us -> 162 us (0.936)
  waiting for transfers between devices: 48 us -> 60.9 us
  local copies, waits for them, and re-layouts: 15.9 us -> 3.72 us
  starting transfers between devices: 45.9 us -> 37.8 us
  Pallas kernels: 61.4 us -> 58.4 us
    ppermute x21, waiting for transfers between devices: 32.5 us -> 47.4 us  [to_corner(): return lax.ppermute(value, 'ex', [(e, e ^ bit) for e in range(n_ex)])]
    unnamed x62 -> x38, local copies, waits for them, and re-layouts: 15.4 us -> 3.28 us
    ppermute x21, starting transfers between devices: 27.4 us -> 21.8 us  [to_corner(): return lax.ppermute(value, 'ex', [(e, e ^ bit) for e in range(n_ex)])]
    pallas_call x1, Pallas kernels: 16.2 us -> 12.8 us  [corner_score(): pl.pallas_call(functools.partial(corner_score_kernel, scale), grid_spec=p...]
    ppermute x12, starting transfers between devices: 17.8 us -> 15.4 us  [to_plane(): lax.ppermute(value, 'ex', [(e, (e + 4 * shift) % n_ex) for e in range(n_e...]
    ppermute x12, waiting for transfers between devices: 13.8 us -> 11.8 us  [to_plane(): lax.ppermute(value, 'ex', [(e, (e + 4 * shift) % n_ex) for e in range(n_e...]
  transfers between devices with their start and end apart: 37 -> 37, of which waited for: 14 -> 19; matrix products, arithmetic and copies ran while one was open for 0% -> 0% of each run, Pallas kernels for 24% -> 26%
where the time goes in v3:
time: 162 us
  waiting for transfers between devices  60.9 us (38%)
  Pallas kernels  58.4 us (36%)
  starting transfers between devices  37.8 us (23%)
  local copies, waits for them, and re-layouts  3.72 us (2%)
    ppermute x21, waiting for transfers between devices, to_corner(): return lax.ppermute(value, 'ex', [(e, e ^ bit) for e in range(n_ex)])  47.4 us
    pallas_call x2, Pallas kernels, block_gram(): pl.pallas_call(functools.partial(block_gram_kernel, len(ties)), grid_spec...  29.3 us
    ppermute x21, starting transfers between devices, to_corner(): return lax.ppermute(value, 'ex', [(e, e ^ bit) for e in range(n_ex)])  21.8 us
    ppermute x12, starting transfers between devices, to_plane(): lax.ppermute(value, 'ex', [(e, (e + 4 * shift) % n_ex) for e in range(n_e...  15.4 us
    pallas_call x1, Pallas kernels, corner_score(): pl.pallas_call(functools.partial(corner_score_kernel, scale), grid_spec=p...  12.8 us
    ppermute x12, waiting for transfers between devices, to_plane(): lax.ppermute(value, 'ex', [(e, (e + 4 * shift) % n_ex) for e in range(n_e...  11.8 us
    pallas_call x1, Pallas kernels, project(): pl.pallas_call(project_kernel, in_specs=[pl.BlockSpec(memory_space=pltpu....  5.58 us
    unnamed x38, local copies, waits for them, and re-layouts  3.28 us
  transfers between devices with their start and end apart: 37, of which 19 were waited for; matrix products, arithmetic and copies ran while one was open for 0% of the time, Pallas kernels for 26%

profile of v3, /device:TPU:0, one launch (start us, length us, event | category | flops | bytes accessed | tf_op | source)
XLA Modules:
  0.0 162.0 jit_solution(12430837791827850138)
XLA Ops:
  0.0 3.0 %collective-permute-start = (bf16[2,512,128]{2,1,0:T(8,128)(2,1)}, bf16[2,512,128]{2,1,0:T(8,128)(2,1)S(1)}, u32[]{:S(2)}, u32[]{:S(2)}) collective-permute-start(bf16[2,512,128]{2,1,0:T(8,128)(2,1)} %own0.1), channel_id=1, source_target_pairs={{0,4},{1,5},{2,6},{3,7},{4,8},{5,9},{6,10},{7,11},{8,12},{9,13},{1... | collective-permute-start | bytes 786440 | tf_op jit(solution)/shard_map/ppermute | solution.py:635
  3.0 2.0 %collective-permute-start.1 = (bf16[2,512,128]{2,1,0:T(8,128)(2,1)}, bf16[2,512,128]{2,1,0:T(8,128)(2,1)S(1)}, u32[]{:S(2)}, u32[]{:S(2)}) collective-permute-start(bf16[2,512,128]{2,1,0:T(8,128)(2,1)} %own0.1), channel_id=1, source_target_pairs={{0,12},{1,13},{2,14},{3,15},{4,0},{5,1},{6,2},{7,3},{8,4},{9,5},{1... | collective-permute-start | bytes 786440 | tf_op jit(solution)/shard_map/ppermute | solution.py:635
  9.2 15.0 %gram.2 = (bf16[2,256,512]{2,1,0:T(8,128)(2,1)S(1)}, bf16[2,256,512]{2,1,0:T(8,128)(2,1)S(1)}, bf16[2,256,512]{2,1,0:T(8,128)(2,1)S(1)}, bf16[2,128,512]{2,1,0:T...) custom-call(s32[6]{0:T(128)S(1)} %stack.147.meta_ref, bf16[3072,4096]{1,0:T(8,128)(2,1)} %refs_7_.1), custom_call_target="tpu_custom_call" | custom-call | flops 9663676416 | bytes 14680064 | tf_op jit(solution)/shard_map/gram/pallas_call | solution.py:279
  24.2 4.2 %collective-permute-done.2.refs_2_ = bf16[2,512,128]{2,1,0:T(8,128)(2,1)S(1)} collective-permute-done((bf16[2,512,128]{2,1,0:T(8,128)(2,1)}, bf16[2,512,128]{2,1,0:T(8,128)(2,1)S(1)}, u32[]{:S(2)}, u32[]{:S(2)}) %collective-permute-start.2) | collective-permute-done | bytes 262176 | tf_op jit(solution)/shard_map/ppermute | solution.py:635
  32.8 5.8 %collective-permute-done.7.from_x = bf16[2,128,512]{2,1,0:T(8,128)(2,1)} collective-permute-done((bf16[2,128,512]{2,1,0:T(8,128)(2,1)}, bf16[2,128,512]{2,1,0:T(8,128)(2,1)}, u32[]{:S(2)}, u32[]{:S(2)}) %collective-permute-start.7) | collective-permute-done | bytes 262176 | tf_op jit(solution)/shard_map/ppermute | solution.py:631
  40.1 14.3 %gram.3 = (bf16[2,256,512]{2,1,0:T(8,128)(2,1)S(1)}, bf16[2,256,512]{2,1,0:T(8,128)(2,1)S(1)}, bf16[2,256,512]{2,1,0:T(8,128)(2,1)S(1)}, bf16[2,128,512]{2,1,0:T...) custom-call(s32[6]{0:T(128)S(1)} %stack.146.meta_ref, bf16[3072,4096]{1,0:T(8,128)(2,1)} %refs_7_.1, ...), custom_call_target="tpu_custom_call" | custom-call | flops 9663676416 | bytes 14680064 | tf_op jit(solution)/shard_map/gram/pallas_call | solution.py:279
  58.2 5.5 %collective-permute-done.5.from_x = bf16[2,128,512]{2,1,0:T(8,128)(2,1)S(1)} collective-permute-done((bf16[2,128,512]{2,1,0:T(8,128)(2,1)S(1)}, bf16[2,128,512]{2,1,0:T(8,128)(2,1)S(1)}, u32[]{:S(2)}, u32[]{:S(2)}) %collective-permute-start.5) | collective-permute-done | bytes 262176 | tf_op jit(solution)/shard_map/ppermute | solution.py:631
  64.2 10.5 %collective-permute-done.6.from_y = bf16[2,128,512]{2,1,0:T(8,128)(2,1)S(1)} collective-permute-done((bf16[2,128,512]{2,1,0:T(8,128)(2,1)S(1)}, bf16[2,128,512]{2,1,0:T(8,128)(2,1)S(1)}, u32[]{:S(2)}, u32[]{:S(2)}) %collective-permute-start.6) | collective-permute-done | bytes 262176 | tf_op jit(solution)/shard_map/ppermute | solution.py:631
  74.9 1.8 %collective-permute-start.13 = (bf16[2,256,512]{2,1,0:T(8,128)(2,1)S(1)}, bf16[2,256,512]{2,1,0:T(8,128)(2,1)S(1)}, u32[]{:S(2)}, u32[]{:S(2)}) collective-permute-start(bf16[2,256,512]{2,1,0:T(8,128)(2,1)S(1)} %get-tuple-element.48), channel_id=1, source_target_pairs={{0,1},{1,0},{2,3},{3,2},{4,5},{5,4},{6,7},{7,6},{8,9},{9,8},{10,11... | collective-permute-start | bytes 1572872 | tf_op jit(solution)/shard_map/ppermute | solution.py:631
  81.1 8.7 %collective-permute-done.13.got_x = bf16[2,256,512]{2,1,0:T(8,128)(2,1)S(1)} collective-permute-done((bf16[2,256,512]{2,1,0:T(8,128)(2,1)S(1)}, bf16[2,256,512]{2,1,0:T(8,128)(2,1)S(1)}, u32[]{:S(2)}, u32[]{:S(2)}) %collective-permute-start.13) | collective-permute-done | bytes 524320 | tf_op jit(solution)/shard_map/ppermute | solution.py:631
  89.8 1.7 %collective-permute-done.14.got_y = bf16[2,256,512]{2,1,0:T(8,128)(2,1)S(1)} collective-permute-done((bf16[2,256,512]{2,1,0:T(8,128)(2,1)S(1)}, bf16[2,256,512]{2,1,0:T(8,128)(2,1)S(1)}, u32[]{:S(2)}, u32[]{:S(2)}) %collective-permute-start.14) | collective-permute-done | bytes 524320 | tf_op jit(solution)/shard_map/ppermute | solution.py:631
  92.4 1.6 %collective-permute-start.17 = (bf16[272,512]{1,0:T(8,128)(2,1)}, bf16[272,512]{1,0:T(8,128)(2,1)}, u32[]{:S(2)}, u32[]{:S(2)}) collective-permute-start(bf16[272,512]{1,0:T(8,128)(2,1)} %close.4), channel_id=1, source_target_pairs={{0,12},{1,13},{2,14},{3,15},{4,0},{5,1},{6,2},{7,3},{8,4},{9,5},{1... | collective-permute-start | bytes 835592 | tf_op jit(solution)/shard_map/ppermute | solution.py:635
  94.3 2.5 %collective-permute-done.20.opp_x = bf16[4,512,128]{2,1,0:T(8,128)(2,1)} collective-permute-done((bf16[4,512,128]{2,1,0:T(8,128)(2,1)}, bf16[4,512,128]{2,1,0:T(8,128)(2,1)}, u32[]{:S(2)}, u32[]{:S(2)}) %collective-permute-start.20) | collective-permute-done | bytes 524320 | tf_op jit(solution)/shard_map/ppermute | solution.py:631
  101.2 5.6 %project.1.total_ref = f32[2,2,128,128]{3,2,1,0:T(8,128)S(1)} custom-call(s32[16]{0:T(128)S(1)} %stack.165.meta_ref, bf16[2,512,128]{2,1,0:T(8,128)(2,1)S(1)} %copy-done.16, bf16[2,3,512,128]{3,2,1,0:T(8,128)(2,1)S(1)} %side_by_side.1.refs_0_.own_b, bf16[2,512,128]{2,1,0:T(8,128)(2,1)S(1)} %collective-permute-done.3.refs_4_.refs_1_.x0, ...), custom_call_target="tpu_custom_call" | custom-call | flops 1073741824 | bytes 12582912 | tf_op jit(solution)/shard_map/project/pallas_call | solution.py:432
  106.8 2.6 %gradients.1 = (f32[4,1024]{1,0:T(4,128)S(1)}, f32[4,1024]{1,0:T(4,128)S(1)}, f32[4,1024]{1,0:T(4,128)S(1)}, f32[4,1024]{1,0:T(4,128)S(1)}) custom-call(s32[4]{0:T(128)S(1)} %pad_add_fusion.1.meta_ref, f32[2,2,128,128]{3,2,1,0:T(8,128)S(1)} %project.1.total_ref, s32[2,128]{1,0:T(2,128)S(1)} %pad_add_fusion.refs_0_, s32[2,128]{1,0:T(2,128)S(1)} %collective-permute-done.22.refs_1_), custom_call_target="tpu_custom_call" | custom-call | flops 536870912 | bytes 524288 | tf_op jit(solution)/shard_map/gradients/pallas_call | solution.py:480
  112.3 6.5 %collective-permute-done.23.across = bf16[272,512]{1,0:T(8,128)(2,1)S(1)} collective-permute-done((bf16[272,512]{1,0:T(8,128)(2,1)S(1)}, bf16[272,512]{1,0:T(8,128)(2,1)S(1)}, u32[]{:S(2)}, u32[]{:S(2)}) %collective-permute-start.23) | collective-permute-done | bytes 278560 | tf_op jit(solution)/shard_map/ppermute | solution.py:631
  120.9 2.2 %collective-permute-start.28 = (f32[4,1024]{1,0:T(4,128)S(1)}, f32[4,1024]{1,0:T(4,128)S(1)}, u32[]{:S(2)}, u32[]{:S(2)}) collective-permute-start(f32[4,1024]{1,0:T(4,128)S(1)} %get-tuple-element.57), channel_id=1, source_target_pairs={{0,8},{1,9},{2,10},{3,11},{4,12},{5,13},{6,14},{7,15},{8,0},{9,1},... | collective-permute-start | bytes 49160 | tf_op jit(solution)/shard_map/ppermute | solution.py:635
  124.9 1.6 %collective-permute-done.27.refs_1_ = f32[4,1024]{1,0:T(4,128)S(1)} collective-permute-done((f32[4,1024]{1,0:T(4,128)S(1)}, f32[4,1024]{1,0:T(4,128)S(1)}, u32[]{:S(2)}, u32[]{:S(2)}) %collective-permute-start.27) | collective-permute-done | bytes 16416 | tf_op jit(solution)/shard_map/ppermute | solution.py:635
  127.1 2.4 %richardson.1 = bf16[16,1024]{1,0:T(8,128)(2,1)S(1)} custom-call(s32[8]{0:T(128)S(1)} %stack.144.meta_ref, bf16[272,512]{1,0:T(8,128)(2,1)S(1)} %close.5.own, bf16[272,512]{1,0:T(8,128)(2,1)S(1)} %collective-permute-done.23.across, bf16[272,512]{1,0:T(8,128)(2,1)S(1)} %collective-permute-done.24.along, bf16[128,512]{1,0:T(8,128)(2,1)S(1)} %collective-permute-done.25.opp_a, ...), custom_call_target="tpu_custom_call" | custom-call | flops 402653184 | bytes 4194304 | tf_op jit(solution)/shard_map/richardson/pallas_call | solution.py:549
  129.5 3.3 %collective-permute-start.32 = (bf16[16,1024]{1,0:T(8,128)(2,1)S(1)}, bf16[16,1024]{1,0:T(8,128)(2,1)S(1)}, u32[]{:S(2)}, u32[]{:S(2)}) collective-permute-start(bf16[16,1024]{1,0:T(8,128)(2,1)S(1)} %richardson.1), channel_id=1, source_target_pairs={{0,12},{1,13},{2,14},{3,15},{4,0},{5,1},{6,2},{7,3},{8,4},{9,5},{1... | collective-permute-start | bytes 98312 | tf_op jit(solution)/shard_map/ppermute | solution.py:635
  134.3 3.2 %collective-permute-done.31 = bf16[16,1024]{1,0:T(8,128)(2,1)S(1)} collective-permute-done((bf16[16,1024]{1,0:T(8,128)(2,1)S(1)}, bf16[16,1024]{1,0:T(8,128)(2,1)S(1)}, u32[]{:S(2)}, u32[]{:S(2)}) %collective-permute-start.31) | collective-permute-done | bytes 32800 | tf_op jit(solution)/shard_map/ppermute | solution.py:635
  144.9 1.7 %collective-permute-done.35.refs_3_ = bf16[4,16,1024]{2,1,0:T(8,128)(2,1)S(1)} collective-permute-done((bf16[4,16,1024]{2,1,0:T(8,128)(2,1)S(1)}, bf16[4,16,1024]{2,1,0:T(8,128)(2,1)S(1)}, u32[]{:S(2)}, u32[]{:S(2)}) %collective-permute-start.35) | collective-permute-done | bytes 131104 | tf_op jit(solution)/shard_map/ppermute | solution.py:631
  146.7 12.8 %score.1 = (f32[32,3072]{1,0:T(8,128)S(1)}, f32[32,3072]{1,0:T(8,128)S(1)}) custom-call(s32[9]{0:T(128)S(1)} %stack.143.meta_ref, bf16[4,16,1024]{2,1,0:T(8,128)(2,1)S(1)} %pad_maximum_fusion.refs_0_, bf16[4,16,1024]{2,1,0:T(8,128)(2,1)S(1)} %collective-permute-done.33.refs_1_, bf16[4,16,1024]{2,1,0:T(8,128)(2,1)S(1)} %collective-permute-done.34.refs_2_, ...), custom_call_target="tpu_custom_call" | custom-call | flops 1610612736 | bytes 25165824 | tf_op jit(solution)/shard_map/score/pallas_call | solution.py:611
  159.5 1.7 %collective-permute-done.36 = f32[32,3072]{1,0:T(8,128)S(1)} collective-permute-done((f32[32,3072]{1,0:T(8,128)S(1)}, f32[32,3072]{1,0:T(8,128)S(1)}, u32[]{:S(2)}, u32[]{:S(2)}) %collective-permute-start.36) | collective-permute-done | bytes 393248 | tf_op jit(solution)/shard_map/ppermute | solution.py:694
  (112 shorter events, 41.5 us)
Async XLA Ops:
  0.0 24.2 %collective-permute-start = (bf16[2,512,128]{2,1,0:T(8,128)(2,1)}, bf16[2,512,128]{2,1,0:T(8,128)(2,1)S(1)}, u32[]{:S(2)}, u32[]{:S(2)}) collective-permute-start(bf16[2,512,128]{2,1,0:T(8,128)(2,1)} %own0.1), channel_id=1, source_target_pairs={{0,4},{1,5},{2,6},{3,7},{4,8},{5,9},{6,10},{7,11},{8,12},{9,13},{1... | collective-permute-start | bytes 786440 | tf_op jit(solution)/shard_map/ppermute | solution.py:635
  3.0 21.2 %collective-permute-start.1 = (bf16[2,512,128]{2,1,0:T(8,128)(2,1)}, bf16[2,512,128]{2,1,0:T(8,128)(2,1)S(1)}, u32[]{:S(2)}, u32[]{:S(2)}) collective-permute-start(bf16[2,512,128]{2,1,0:T(8,128)(2,1)} %own0.1), channel_id=1, source_target_pairs={{0,12},{1,13},{2,14},{3,15},{4,0},{5,1},{6,2},{7,3},{8,4},{9,5},{1... | collective-permute-start | bytes 786440 | tf_op jit(solution)/shard_map/ppermute | solution.py:635
  5.1 23.4 %collective-permute-start.2 = (bf16[2,512,128]{2,1,0:T(8,128)(2,1)}, bf16[2,512,128]{2,1,0:T(8,128)(2,1)S(1)}, u32[]{:S(2)}, u32[]{:S(2)}) collective-permute-start(bf16[2,512,128]{2,1,0:T(8,128)(2,1)} %own0.1), channel_id=1, source_target_pairs={{0,8},{1,9},{2,10},{3,11},{4,12},{5,13},{6,14},{7,15},{8,0},{9,1},... | collective-permute-start | bytes 786440 | tf_op jit(solution)/shard_map/ppermute | solution.py:635
  6.1 22.4 %collective-permute-start.3 = (bf16[2,512,128]{2,1,0:T(8,128)(2,1)}, bf16[2,512,128]{2,1,0:T(8,128)(2,1)S(1)}, u32[]{:S(2)}, u32[]{:S(2)}) collective-permute-start(bf16[2,512,128]{2,1,0:T(8,128)(2,1)} %own0.1), channel_id=1, source_target_pairs={{0,1},{1,0},{2,3},{3,2},{4,5},{5,4},{6,7},{7,6},{8,9},{9,8},{10,11... | collective-permute-start | bytes 786440 | tf_op jit(solution)/shard_map/ppermute | solution.py:631
  7.6 20.9 %collective-permute-start.4 = (bf16[2,512,128]{2,1,0:T(8,128)(2,1)}, bf16[2,512,128]{2,1,0:T(8,128)(2,1)S(1)}, u32[]{:S(2)}, u32[]{:S(2)}) collective-permute-start(bf16[2,512,128]{2,1,0:T(8,128)(2,1)} %own0.1), channel_id=1, source_target_pairs={{0,2},{1,3},{2,0},{3,1},{4,6},{5,7},{6,4},{7,5},{8,10},{9,11},{10,... | collective-permute-start | bytes 786440 | tf_op jit(solution)/shard_map/ppermute | solution.py:631
  28.5 27.4 %collective-permute-start.9 = (bf16[128,8192]{1,0:T(8,128)(2,1)}, bf16[128,8192]{1,0:T(8,128)(2,1)S(1)}, u32[]{:S(2)}, u32[]{:S(2)}) collective-permute-start(bf16[128,8192]{1,0:T(8,128)(2,1)} %bitcast.10.refs_0_), channel_id=1, source_target_pairs={{0,16},{16,0},{1,17},{17,1},{2,18},{18,2},{3,19},{19,3},{4,20},{20... | collective-permute-start | bytes 6291464 | tf_op jit(solution)/shard_map/ppermute | solution.py:134
  28.6 27.3 %collective-permute-start.10 = (bf16[128,8192]{1,0:T(8,128)(2,1)}, bf16[128,8192]{1,0:T(8,128)(2,1)}, u32[]{:S(2)}, u32[]{:S(2)}) collective-permute-start(bf16[128,8192]{1,0:T(8,128)(2,1)} %bitcast.11.refs_2_), channel_id=1, source_target_pairs={{0,16},{16,0},{1,17},{17,1},{2,18},{18,2},{3,19},{19,3},{4,20},{20... | collective-permute-start | bytes 6291464 | tf_op jit(solution)/shard_map/ppermute | solution.py:134
  29.1 9.5 %collective-permute-start.7 = (bf16[2,128,512]{2,1,0:T(8,128)(2,1)}, bf16[2,128,512]{2,1,0:T(8,128)(2,1)}, u32[]{:S(2)}, u32[]{:S(2)}) collective-permute-start(bf16[2,128,512]{2,1,0:T(8,128)(2,1)} %get-tuple-element.41), channel_id=1, source_target_pairs={{0,1},{1,0},{2,3},{3,2},{4,5},{5,4},{6,7},{7,6},{8,9},{9,8},{10,11... | collective-permute-start | bytes 786440 | tf_op jit(solution)/shard_map/ppermute | solution.py:631
  30.6 23.8 %collective-permute-start.8 = (bf16[2,128,512]{2,1,0:T(8,128)(2,1)}, bf16[2,128,512]{2,1,0:T(8,128)(2,1)}, u32[]{:S(2)}, u32[]{:S(2)}) collective-permute-start(bf16[2,128,512]{2,1,0:T(8,128)(2,1)} %get-tuple-element.42), channel_id=1, source_target_pairs={{0,2},{1,3},{2,0},{3,1},{4,6},{5,7},{6,4},{7,5},{8,10},{9,11},{10,... | collective-permute-start | bytes 786440 | tf_op jit(solution)/shard_map/ppermute | solution.py:631
  32.2 45.0 %collective-permute-start.18 = (bf16[2,3,512,128]{3,2,1,0:T(8,128)(2,1)S(1)}, bf16[2,3,512,128]{3,2,1,0:T(8,128)(2,1)S(1)}, u32[]{:S(2)}, u32[]{:S(2)}) collective-permute-start(bf16[2,3,512,128]{3,2,1,0:T(8,128)(2,1)S(1)} %side_by_side.1.refs_0_.own_b), channel_id=1, source_target_pairs={{0,1},{1,0},{2,3},{3,2},{4,5},{5,4},{6,7},{7,6},{8,9},{9,8},{10,11... | collective-permute-start | bytes 2359304 | tf_op jit(solution)/shard_map/ppermute | solution.py:631
  38.6 38.6 %collective-permute-start.19 = (bf16[2,3,512,128]{3,2,1,0:T(8,128)(2,1)S(1)}, bf16[2,3,512,128]{3,2,1,0:T(8,128)(2,1)S(1)}, u32[]{:S(2)}, u32[]{:S(2)}) collective-permute-start(bf16[2,3,512,128]{3,2,1,0:T(8,128)(2,1)S(1)} %side_by_side.1.refs_0_.own_b), channel_id=1, source_target_pairs={{0,2},{1,3},{2,0},{3,1},{4,6},{5,7},{6,4},{7,5},{8,10},{9,11},{10,... | collective-permute-start | bytes 2359304 | tf_op jit(solution)/shard_map/ppermute | solution.py:631
  54.4 9.3 %collective-permute-start.5 = (bf16[2,128,512]{2,1,0:T(8,128)(2,1)S(1)}, bf16[2,128,512]{2,1,0:T(8,128)(2,1)S(1)}, u32[]{:S(2)}, u32[]{:S(2)}) collective-permute-start(bf16[2,128,512]{2,1,0:T(8,128)(2,1)S(1)} %get-tuple-element.37), channel_id=1, source_target_pairs={{0,1},{1,0},{2,3},{3,2},{4,5},{5,4},{6,7},{7,6},{8,9},{9,8},{10,11... | collective-permute-start | bytes 786440 | tf_op jit(solution)/shard_map/ppermute | solution.py:631
  57.1 17.6 %collective-permute-start.11 = (bf16[2,256,512]{2,1,0:T(8,128)(2,1)S(1)}, bf16[2,256,512]{2,1,0:T(8,128)(2,1)S(1)}, u32[]{:S(2)}, u32[]{:S(2)}) collective-permute-start(bf16[2,256,512]{2,1,0:T(8,128)(2,1)S(1)} %get-tuple-element.46.tie), channel_id=1, source_target_pairs={{0,1},{1,0},{2,3},{3,2},{4,5},{5,4},{6,7},{7,6},{8,9},{9,8},{10,11... | collective-permute-start | bytes 1572872 | tf_op jit(solution)/shard_map/ppermute | solution.py:631
  57.7 17.0 %collective-permute-start.12 = (bf16[2,256,512]{2,1,0:T(8,128)(2,1)S(1)}, bf16[2,256,512]{2,1,0:T(8,128)(2,1)S(1)}, u32[]{:S(2)}, u32[]{:S(2)}) collective-permute-start(bf16[2,256,512]{2,1,0:T(8,128)(2,1)S(1)} %get-tuple-element.47), channel_id=1, source_target_pairs={{0,2},{1,3},{2,0},{3,1},{4,6},{5,7},{6,4},{7,5},{8,10},{9,11},{10,... | collective-permute-start | bytes 1572872 | tf_op jit(solution)/shard_map/ppermute | solution.py:631
  63.7 11.0 %collective-permute-start.6 = (bf16[2,128,512]{2,1,0:T(8,128)(2,1)S(1)}, bf16[2,128,512]{2,1,0:T(8,128)(2,1)S(1)}, u32[]{:S(2)}, u32[]{:S(2)}) collective-permute-start(bf16[2,128,512]{2,1,0:T(8,128)(2,1)S(1)} %get-tuple-element.38), channel_id=1, source_target_pairs={{0,2},{1,3},{2,0},{3,1},{4,6},{5,7},{6,4},{7,5},{8,10},{9,11},{10,... | collective-permute-start | bytes 786440 | tf_op jit(solution)/shard_map/ppermute | solution.py:631
  74.9 14.9 %collective-permute-start.13 = (bf16[2,256,512]{2,1,0:T(8,128)(2,1)S(1)}, bf16[2,256,512]{2,1,0:T(8,128)(2,1)S(1)}, u32[]{:S(2)}, u32[]{:S(2)}) collective-permute-start(bf16[2,256,512]{2,1,0:T(8,128)(2,1)S(1)} %get-tuple-element.48), channel_id=1, source_target_pairs={{0,1},{1,0},{2,3},{3,2},{4,5},{5,4},{6,7},{7,6},{8,9},{9,8},{10,11... | collective-permute-start | bytes 1572872 | tf_op jit(solution)/shard_map/ppermute | solution.py:631
  76.6 14.9 %collective-permute-start.14 = (bf16[2,256,512]{2,1,0:T(8,128)(2,1)S(1)}, bf16[2,256,512]{2,1,0:T(8,128)(2,1)S(1)}, u32[]{:S(2)}, u32[]{:S(2)}) collective-permute-start(bf16[2,256,512]{2,1,0:T(8,128)(2,1)S(1)} %get-tuple-element.49), channel_id=1, source_target_pairs={{0,2},{1,3},{2,0},{3,1},{4,6},{5,7},{6,4},{7,5},{8,10},{9,11},{10,... | collective-permute-start | bytes 1572872 | tf_op jit(solution)/shard_map/ppermute | solution.py:631
  78.3 18.4 %collective-permute-start.20 = (bf16[4,512,128]{2,1,0:T(8,128)(2,1)}, bf16[4,512,128]{2,1,0:T(8,128)(2,1)}, u32[]{:S(2)}, u32[]{:S(2)}) collective-permute-start(bf16[4,512,128]{2,1,0:T(8,128)(2,1)} %get-tuple-element.53), channel_id=1, source_target_pairs={{0,1},{1,0},{2,3},{3,2},{4,5},{5,4},{6,7},{7,6},{8,9},{9,8},{10,11... | collective-permute-start | bytes 1572872 | tf_op jit(solution)/shard_map/ppermute | solution.py:631
  78.6 19.3 %collective-permute-start.21 = (bf16[4,512,128]{2,1,0:T(8,128)(2,1)}, bf16[4,512,128]{2,1,0:T(8,128)(2,1)}, u32[]{:S(2)}, u32[]{:S(2)}) collective-permute-start(bf16[4,512,128]{2,1,0:T(8,128)(2,1)} %get-tuple-element.54), channel_id=1, source_target_pairs={{0,2},{1,3},{2,0},{3,1},{4,6},{5,7},{6,4},{7,5},{8,10},{9,11},{10,... | collective-permute-start | bytes 1572872 | tf_op jit(solution)/shard_map/ppermute | solution.py:631
  81.1 28.4 %collective-permute-start.15 = (bf16[272,512]{1,0:T(8,128)(2,1)}, bf16[272,512]{1,0:T(8,128)(2,1)}, u32[]{:S(2)}, u32[]{:S(2)}) collective-permute-start(bf16[272,512]{1,0:T(8,128)(2,1)} %get-tuple-element.51), channel_id=1, source_target_pairs={{0,4},{1,5},{2,6},{3,7},{4,8},{5,9},{6,10},{7,11},{8,12},{9,13},{1... | collective-permute-start | bytes 835592 | tf_op jit(solution)/shard_map/ppermute | solution.py:635
  89.8 19.6 %collective-permute-start.16 = (bf16[272,512]{1,0:T(8,128)(2,1)}, bf16[272,512]{1,0:T(8,128)(2,1)}, u32[]{:S(2)}, u32[]{:S(2)}) collective-permute-start(bf16[272,512]{1,0:T(8,128)(2,1)} %get-tuple-element.52), channel_id=1, source_target_pairs={{0,8},{1,9},{2,10},{3,11},{4,12},{5,13},{6,14},{7,15},{8,0},{9,1},... | collective-permute-start | bytes 835592 | tf_op jit(solution)/shard_map/ppermute | solution.py:635
  92.4 17.0 %collective-permute-start.17 = (bf16[272,512]{1,0:T(8,128)(2,1)}, bf16[272,512]{1,0:T(8,128)(2,1)}, u32[]{:S(2)}, u32[]{:S(2)}) collective-permute-start(bf16[272,512]{1,0:T(8,128)(2,1)} %close.4), channel_id=1, source_target_pairs={{0,12},{1,13},{2,14},{3,15},{4,0},{5,1},{6,2},{7,3},{8,4},{9,5},{1... | collective-permute-start | bytes 835592 | tf_op jit(solution)/shard_map/ppermute | solution.py:635
  96.7 10.0 %collective-permute-start.22 = (s32[2,128]{1,0:T(2,128)S(1)}, s32[2,128]{1,0:T(2,128)S(1)}, u32[]{:S(2)}, u32[]{:S(2)}) collective-permute-start(s32[2,128]{1,0:T(2,128)S(1)} %pad_add_fusion.refs_0_), channel_id=1, source_target_pairs={{0,16},{16,0},{1,17},{17,1},{2,18},{18,2},{3,19},{19,3},{4,20},{20... | collective-permute-start | bytes 3080 | tf_op jit(solution)/shard_map/ppermute | solution.py:134
  111.8 8.3 %collective-permute-start.24 = (bf16[272,512]{1,0:T(8,128)(2,1)S(1)}, bf16[272,512]{1,0:T(8,128)(2,1)S(1)}, u32[]{:S(2)}, u32[]{:S(2)}) collective-permute-start(bf16[272,512]{1,0:T(8,128)(2,1)S(1)} %close.5.own), channel_id=1, source_target_pairs={{0,2},{1,3},{2,0},{3,1},{4,6},{5,7},{6,4},{7,5},{8,10},{9,11},{10,... | collective-permute-start | bytes 835592 | tf_op jit(solution)/shard_map/ppermute | solution.py:631
  (32 other events, 230.6 us)
